TPU v7x, 128 devices: a whole 4x4x4 slice. The times are simulated.
128 devices in a mesh: range: 32 (over z, x, core), cross: 4 (over y).
Axes of the slice: x: 4, y: 4, z: 4, core: 2. Of those that a mesh axis runs over, the one named last changes fastest.
Arguments:
- surface_field: bfloat16 [131072, 1024], P(('range', 'cross')), may hold values from -6 to 6
- point_count: int32 [128], P(('range', 'cross')), may hold values from 512 to 1024, as said below
- far_rank: int32 [128, 128], P(('range', 'cross')), may hold values from 4 to 16, as said below
- source_factor: bfloat16 [2, 2048, 131072], P(None, None, ('range', 'cross')), may hold values from -0.1875 to 0.1875
- target_factor: bfloat16 [2, 131072, 2048], P(None, ('range', 'cross')), may hold values from -0.5 to 0.5
- near_blocks: bfloat16 [2, 131072, 3, 128], P(None, ('range', 'cross')), may hold values from -0.3125 to 0.3125
- near_index: int32 [1024, 3], P(('range', 'cross')), may hold values from 0 to 11
Outputs:
- scattered: bfloat16 [131072, 1024], P(('range', 'cross'))
Inputs may be any that keep to these rules, and one draw needn't show every extreme that they name: `point_count`: each count lies between half a box and a full box; some box is full. `far_rank`: every source box has a pair of full rank 16.
All inputs are finite; a program needn't handle non-finite values.
Results may differ from a plain program's by a relative error of at most 0.0043.
Values may be sent and summed in bfloat16 or wider, within the bound.
No kernel may reach another device: no remote copies, remote signals or barrier semaphores. Data moves between devices by JAX's collectives and lax.ppermute only.
A program may use at most 128 MiB of HBM per device.

v0:
```python
import jax
import jax.numpy as jnp
from jax import lax
from jax.sharding import PartitionSpec as P

RANK = 16
NEAR_B = 128
NB = 3
HALO_BLK = 2


def with_halo(block, sides, width):
    for axis, dim in sides:
        count = lax.axis_size(axis)
        forward = [(i, i + 1) for i in range(count - 1)]
        backward = [(target, source) for source, target in forward]
        low = lax.ppermute(
            lax.slice_in_dim(block, block.shape[dim] - width, None, axis=dim), axis, forward
        )
        high = lax.ppermute(lax.slice_in_dim(block, 0, width, axis=dim), axis, backward)
        block = jnp.concatenate([low, block, high], axis=dim)
    return block


def rotate(block):
    half = block.shape[-1] // 2
    return jnp.concatenate([-block[..., half:], block[..., :half]], axis=-1)


def shards(
    surface_field, point_count, far_rank, source_factor, target_factor, near_blocks, near_index
):
    points = surface_field.shape[0]
    width_cols = surface_field.shape[1]
    boxes = far_rank.shape[1]
    live_rows = (lax.iota(jnp.int32, points) < point_count[0])[:, None]
    field = surface_field * live_rows.astype(jnp.bfloat16)
    coeffs = jnp.dot(source_factor[0], field, preferred_element_type=jnp.float32)
    coeffs = coeffs + jnp.dot(source_factor[1], rotate(field), preferred_element_type=jnp.float32)
    keep = (lax.iota(jnp.int32, RANK)[None, :] < far_rank[0][:, None]).reshape(boxes * RANK, 1)
    coeffs = jnp.where(keep, coeffs, jnp.float32(0.0)).astype(jnp.bfloat16)
    arrived = lax.all_to_all(coeffs, ("range", "cross"), split_axis=0, concat_axis=0, tiled=True)
    far = jnp.dot(target_factor[0], arrived, preferred_element_type=jnp.float32)
    far = far + jnp.dot(target_factor[1], rotate(arrived), preferred_element_type=jnp.float32)
    rim = HALO_BLK * NEAR_B
    window = with_halo(field, (("cross", 0),), rim)
    window_blocks = window.reshape(-1, NEAR_B, width_cols)
    picked = window_blocks[near_index]
    blocks_here = points // NEAR_B
    mats = near_blocks.reshape(2, blocks_here, NEAR_B, NB, NEAR_B)
    near = jnp.einsum("bink,bnkc->bic", mats[0], picked, preferred_element_type=jnp.float32)
    near = near + jnp.einsum(
        "bink,bnkc->bic", mats[1], rotate(picked), preferred_element_type=jnp.float32
    )
    near = near.reshape(points, width_cols)
    return ((near + far) * live_rows.astype(jnp.float32)).astype(jnp.bfloat16)


def solution(mesh):
    return jax.shard_map(
        shards,
        mesh=mesh,
        in_specs=(
            P(("range", "cross"), None),
            P(("range", "cross")),
            P(("range", "cross"), None),
            P(None, None, ("range", "cross")),
            P(None, ("range", "cross"), None),
            P(None, ("range", "cross"), None, None),
            P(("range", "cross"), None),
        ),
        out_specs=P(("range", "cross"), None),
        check_vma=False,
    )
```

profile of v0, /device:TPU:1, one launch (start us, length us, event | category | flops | bytes accessed | tf_op | source)
XLA Modules:
  0.0 135.7 jit_solution(10138621953766738497)
XLA Ops:
  0.7 0.0 copy-start.7
  0.7 1.8 %broadcast_multiply_fusion = bf16[1024,1024]{1,0:T(8,128)(2,1)S(1)} fusion(bf16[1024,1024]{1,0:T(8,128)(2,1)} %param.7, bf16[1024]{0:T(1024)(128)(2,1)S(1)} %fusion.34), kind=kLoop, calls=%fused_computation.33 | loop fusion | flops 1048576 | bytes 4196352 | tf_op jit(solution)/shard_map/mul | solution.py:37
  2.5 0.0 copy-start
  2.5 1.2 slice_negate_fusion.2
  3.7 0.0 copy-done.7
  3.7 0.1 iota_compare_fusion
  3.8 0.1 lt.45
  3.9 6.7 %fusion.14 = f32[1024,2048]{1,0:T(8,128)S(1)} fusion(bf16[2,2048,1024]{2,1,0:T(8,128)(2,1)} %param.10, bf16[1024,512]{1,0:T(8,128)(2,1)} %get-tuple-element.10, bf16[1024,512]{1,0:T(8,128)(2,1)S(1)} %get-tuple-element.9), kind=kOutput, calls=%fused_computation.17 | convolution fusion | flops 4299161600 | bytes 14680064 | tf_op jit(solution)/shard_map/dot_general | solution.py:39
  10.6 8.5 %fusion.4 = bf16[2048,1024]{0,1:T(8,128)(2,1)} fusion(f32[1024,2048]{1,0:T(8,128)S(1)} %fusion.14, pred[2048]{0:T(1024)(128)(4,1)S(1)} %lt.45, bf16[1024,1024]{1,0:T(8,128)(2,1)S(1)} %broadcast_multiply_fusion, bf16[2,2048,1024]{2,1,0:T(8,128)(2,1)} %param.10), kind=kOutput, calls=%fused_computation.6 | convolution fusion | flops 4301258752 | bytes 18876416 | tf_op jit(solution)/shard_map/dot_general | solution.py:38
  19.1 6.4 %copy.14 = bf16[2048,1024]{1,0:T(8,128)(2,1)} copy(bf16[2048,1024]{0,1:T(8,128)(2,1)} %fusion.4) | data formatting | bytes 8388608 | tf_op jit(solution)/shard_map/convert_element_type | solution.py:41
  25.5 0.0 copy-start.6
  25.5 12.0 %all-to-all-start = ((bf16[128,16,1024]{2,1,0:T(8,128)(2,1)}), bf16[128,16,1024]{2,1,0:T(8,128)(2,1)}, u32[]{:S(2)}, u32[]{:S(2)}) async-start(bf16[128,16,1024]{2,1,0:T(8,128)(2,1)} %bitcast.51), calls=%async_computation | async-start | bytes 8388608 | tf_op jit(solution)/shard_map/all_to_all | solution.py:42
  37.4 0.0 copy-done
  37.5 0.1 fusion.38
  37.5 3.3 %collective-permute-start = (bf16[256,1024]{1,0:T(8,128)(2,1)S(1)}, bf16[256,1024]{1,0:T(8,128)(2,1)S(1)}, u32[]{:S(2)}, u32[]{:S(2)}) collective-permute-start(bf16[256,1024]{1,0:T(8,128)(2,1)S(1)} %get-tuple-element.11), channel_id=1, source_target_pairs={{0,1},{1,2},{2,3},{4,5},{5,6},{6,7},{8,9},{9,10},{10,11},{12,13},{... | collective-permute-start | bytes 1572872 | tf_op jit(solution)/shard_map/ppermute | solution.py:17
  40.9 1.5 %collective-permute-start.1 = (bf16[256,1024]{1,0:T(8,128)(2,1)S(1)}, bf16[256,1024]{1,0:T(8,128)(2,1)}, u32[]{:S(2)}, u32[]{:S(2)}) collective-permute-start(bf16[256,1024]{1,0:T(8,128)(2,1)S(1)} %get-tuple-element.12), channel_id=1, source_target_pairs={{1,0},{2,1},{3,2},{5,4},{6,5},{7,6},{9,8},{10,9},{11,10},{13,12},{... | collective-permute-start | bytes 1572872 | tf_op jit(solution)/shard_map/ppermute | solution.py:20
  42.3 0.0 copy-done.6
  42.4 0.1 copy.11
  42.4 0.1 reshape.43
  42.5 0.0 copy-start.1
  42.5 2.8 %fusion.39 = (bf16[1,1024,3,128]{3,1,2,0:T(8,128)(2,1)}, bf16[1,1024,3,128]{3,1,2,0:T(8,128)(2,1)}) fusion(bf16[2,1024,3,128]{3,1,2,0:T(8,128)(2,1)} %param.12), kind=kLoop, calls=%fused_computation.46 | loop fusion | bytes 3145728 | tf_op jit(solution)/shard_map/slice | solution.py:51
  45.4 46.4 %collective-permute-done = bf16[256,1024]{1,0:T(8,128)(2,1)S(1)} collective-permute-done((bf16[256,1024]{1,0:T(8,128)(2,1)S(1)}, bf16[256,1024]{1,0:T(8,128)(2,1)S(1)}, u32[]{:S(2)}, u32[]{:S(2)}) %collective-permute-start) | collective-permute-done | bytes 524320 | tf_op jit(solution)/shard_map/ppermute | solution.py:17
  91.8 0.0 copy-start.5
  91.8 0.8 copy-done.5
  92.6 2.3 %collective-permute-done.1 = bf16[256,1024]{1,0:T(8,128)(2,1)} collective-permute-done((bf16[256,1024]{1,0:T(8,128)(2,1)S(1)}, bf16[256,1024]{1,0:T(8,128)(2,1)}, u32[]{:S(2)}, u32[]{:S(2)}) %collective-permute-start.1) | collective-permute-done | bytes 524320 | tf_op jit(solution)/shard_map/ppermute | solution.py:20
  94.8 0.0 copy-done.1
  94.8 1.4 %pad_maximum_fusion = bf16[1536,1024]{1,0:T(8,128)(2,1)S(1)} fusion(bf16[256,1024]{1,0:T(8,128)(2,1)} %collective-permute-done.1, bf16[1024,1024]{1,0:T(8,128)(2,1)S(1)} %copy-done.1, bf16[256,1024]{1,0:T(8,128)(2,1)} %copy-done.5), kind=kLoop, calls=%fused_computation.27 | loop fusion | flops 9437184 | bytes 6291456 | tf_op jit(solution)/shard_map/concatenate | solution.py:21
  96.3 4.4 %gather_fusion = bf16[24,128,1024]{2,1,0:T(8,128)(2,1)} fusion(bf16[12,128,1024]{2,1,0:T(8,128)(2,1)S(1)} %bitcast.50, s32[1024]{0:T(1024)S(1)} %pad_clamp_fusion), kind=kCustom, calls=%fused_computation | custom fusion | bytes 12583008 | tf_op jit(solution)/shard_map/gather | solution.py:48
  100.7 0.0 copy-start.4
  100.7 3.3 %slice_negate_fusion = (bf16[8,3,128,512]{3,2,1,0:T(8,128)(2,1)S(1)}, bf16[8,3,128,512]{3,2,1,0:T(8,128)(2,1)S(1)}) fusion(bf16[8,3,128,1024]{3,2,1,0:T(8,128)(2,1)} %bitcast.46), kind=kLoop, calls=%fused_computation.26 | loop fusion | flops 1572864 | bytes 12582912 | tf_op jit(solution)/shard_map/neg | solution.py:27
  104.0 0.0 slice-start
  104.0 0.0 copy-done.4
  104.0 0.0 slice-start.1
  104.0 0.0 copy-start.3
  104.0 1.5 %fusion = f32[8,1024,128,1]{1,2,3,0:T(8,128)S(1)} fusion(bf16[8,3,128,512]{3,2,1,0:T(8,128)(2,1)S(1)} %get-tuple-element.6, bf16[8,3,128,512]{3,2,1,0:T(8,128)(2,1)S(1)} %get-tuple-element.5, bf16[8,128,3,128]{3,1,0,2:T(8,128)(2,1)S(1)} %bitcast.54), kind=kOutput, calls=%fused_computation.2 | convolution fusion | flops 817889280 | bytes 11272192 | tf_op jit(solution)/shard_map/bink,bnkc->bic/dot_general | solution.py:52
  105.5 0.7 slice-done
  106.2 0.7 slice-done.1
  106.9 0.1 copy-done.3
  107.0 3.2 %bitcast_add_fusion.1 = f32[8,1024,128]{1,2,0:T(8,128)} fusion(f32[8,1024,128,1]{1,2,3,0:T(8,128)S(1)} %fusion, bf16[8,3,128,1024]{3,2,1,0:T(8,128)(2,1)S(1)} %bitcast.49, bf16[8,128,3,128]{3,1,0,2:T(8,128)(2,1)S(1)} %bitcast.53), kind=kOutput, calls=%fused_computation.21 | convolution fusion | flops 806354944 | bytes 15466496 | tf_op jit(solution)/shard_map/bink,bnkc->bic/dot_general | solution.py:51
  110.2 5.4 %copy.15 = f32[1024,1024]{0,1:T(8,128)} copy(f32[1024,1024]{1,0:T(8,128)} %bitcast.52) | data formatting | bytes 8388608 | tf_op jit(solution)/shard_map/reshape | solution.py:55
  115.6 0.0 all-to-all-done
  115.6 2.5 %slice_negate_fusion.1 = (bf16[2048,512]{1,0:T(8,128)(2,1)S(1)}, bf16[2048,512]{1,0:T(8,128)(2,1)S(1)}) fusion(bf16[2048,1024]{1,0:T(8,128)(2,1)} %bitcast.16), kind=kLoop, calls=%fused_computation.28 | loop fusion | flops 1048576 | bytes 8388608 | tf_op jit(solution)/shard_map/neg | solution.py:27
  118.1 0.0 copy-start.2
  118.1 7.8 %fusion.12 = f32[1024,1024]{1,0:T(8,128)S(1)} fusion(bf16[2048,1024]{1,0:T(8,128)(2,1)} %bitcast.16, bf16[2,1024,2048]{2,1,0:T(8,128)(2,1)} %param.11), kind=kOutput, calls=%fused_computation.15 | convolution fusion | flops 4294967296 | bytes 12582912 | tf_op jit(solution)/shard_map/dot_general | solution.py:43
  125.8 0.0 copy-done.2
  125.9 7.2 %fusion.10 = bf16[1024,1024]{0,1:T(8,128)(2,1)S(1)} fusion(f32[1024,1024]{0,1:T(8,128)S(1)} %copy-done.2, f32[1024,1024]{1,0:T(8,128)S(1)} %fusion.12, f32[1024]{0:T(1024)S(1)} %fusion.33, bf16[2,1024,2048]{2,1,0:T(8,128)(2,1)} %param.11, bf16[2048,512]{1,0:T(8,128)(2,1)S(1)} %get-tuple-element.8, bf16[2048,512]{1,0:T(8,128)(2,1)S(1)} %get-tuple-element.7), kind=kOutput, calls=%fused_computation.13 | convolution fusion | flops 4307550208 | bytes 18878464 | tf_op jit(solution)/shard_map/dot_general | solution.py:44
  133.1 2.6 %copy.16 = bf16[1024,1024]{1,0:T(8,128)(2,1)} copy(bf16[1024,1024]{0,1:T(8,128)(2,1)S(1)} %fusion.10) | data formatting | bytes 4194304 | tf_op jit(solution)/shard_map/convert_element_type | solution.py:56
  (5 shorter events, 0.0 us)
Async XLA Ops:
  0.7 3.1 %copy-start.7 = (s32[1,128]{1,0:T(1,128)S(1)}, s32[1,128]{1,0:T(1,128)}, u32[]{:S(2)}) copy-start(s32[1,128]{1,0:T(1,128)} %param.9) | copy-start | bytes 1540
  2.5 35.0 %copy-start = (bf16[1024,1024]{1,0:T(8,128)(2,1)}, bf16[1024,1024]{1,0:T(8,128)(2,1)S(1)}, u32[]{:S(2)}) copy-start(bf16[1024,1024]{1,0:T(8,128)(2,1)S(1)} %broadcast_multiply_fusion) | copy-start | bytes 6291460
  25.5 16.9 %copy-start.6 = (s32[8,3]{0,1:T(4,128)S(1)}, s32[8,3]{0,1:T(4,128)}, u32[]{:S(2)}) copy-start(s32[8,3]{0,1:T(4,128)} %param.13) | copy-start | bytes 292
  25.5 90.1 %all-to-all-start = ((bf16[128,16,1024]{2,1,0:T(8,128)(2,1)}), bf16[128,16,1024]{2,1,0:T(8,128)(2,1)}, u32[]{:S(2)}, u32[]{:S(2)}) async-start(bf16[128,16,1024]{2,1,0:T(8,128)(2,1)} %bitcast.51), calls=%async_computation | async-start | bytes 8388608 | tf_op jit(solution)/shard_map/all_to_all | solution.py:42
  37.5 54.2 %collective-permute-start = (bf16[256,1024]{1,0:T(8,128)(2,1)S(1)}, bf16[256,1024]{1,0:T(8,128)(2,1)S(1)}, u32[]{:S(2)}, u32[]{:S(2)}) collective-permute-start(bf16[256,1024]{1,0:T(8,128)(2,1)S(1)} %get-tuple-element.11), channel_id=1, source_target_pairs={{0,1},{1,2},{2,3},{4,5},{5,6},{6,7},{8,9},{9,10},{10,11},{12,13},{... | collective-permute-start | bytes 1572872 | tf_op jit(solution)/shard_map/ppermute | solution.py:17
  40.9 54.0 %collective-permute-start.1 = (bf16[256,1024]{1,0:T(8,128)(2,1)S(1)}, bf16[256,1024]{1,0:T(8,128)(2,1)}, u32[]{:S(2)}, u32[]{:S(2)}) collective-permute-start(bf16[256,1024]{1,0:T(8,128)(2,1)S(1)} %get-tuple-element.12), channel_id=1, source_target_pairs={{1,0},{2,1},{3,2},{5,4},{6,5},{7,6},{9,8},{10,9},{11,10},{13,12},{... | collective-permute-start | bytes 1572872 | tf_op jit(solution)/shard_map/ppermute | solution.py:20
  42.5 52.3 %copy-start.1 = (bf16[1024,1024]{1,0:T(8,128)(2,1)S(1)}, bf16[1024,1024]{1,0:T(8,128)(2,1)}, u32[]{:S(2)}) copy-start(bf16[1024,1024]{1,0:T(8,128)(2,1)} %copy-done) | copy-start | bytes 6291460
  91.8 0.8 copy-start.5
  100.7 3.3 %copy-start.4 = (bf16[1,1024,3,128]{3,1,2,0:T(8,128)(2,1)S(1)}, bf16[1,1024,3,128]{3,1,2,0:T(8,128)(2,1)}, u32[]{:S(2)}) copy-start(bf16[1,1024,3,128]{3,1,2,0:T(8,128)(2,1)} %get-tuple-element.14) | copy-start | bytes 2359300
  104.0 2.2 %slice-start = ((s8[6291456]{0:T(1024)(128)(4,1)}), s8[4194304]{0:T(1024)(128)(4,1)S(1)}, s32[]{:S(2)}) async-start(s8[6291456]{0:T(1024)(128)(4,1)} %bitcast.47), calls=%async_computation.1 | async-start | bytes 8388608
  104.0 2.9 %slice-start.1 = ((s8[6291456]{0:T(1024)(128)(4,1)}), s8[2097152]{0:T(1024)(128)(4,1)S(1)}, s32[]{:S(2)}) async-start(s8[6291456]{0:T(1024)(128)(4,1)} %bitcast.47), calls=%async_computation.2 | async-start | bytes 4194304
  104.0 3.0 %copy-start.3 = (bf16[1,1024,3,128]{3,1,2,0:T(8,128)(2,1)S(1)}, bf16[1,1024,3,128]{3,1,2,0:T(8,128)(2,1)}, u32[]{:S(2)}) copy-start(bf16[1,1024,3,128]{3,1,2,0:T(8,128)(2,1)} %get-tuple-element.13) | copy-start | bytes 2359300
  118.1 7.8 %copy-start.2 = (f32[1024,1024]{0,1:T(8,128)S(1)}, f32[1024,1024]{0,1:T(8,128)}, u32[]{:S(2)}) copy-start(f32[1024,1024]{0,1:T(8,128)} %copy.15) | copy-start | bytes 12582916
where the time goes:
time: 136 us
  waiting for transfers between devices  48.6 us (36%)
  matrix products  34.8 us (26%)
  local copies, waits for them, and re-layouts  24.2 us (18%)
  starting transfers between devices  16.8 us (12%)
  other arithmetic  10.4 us (8%)
    ppermute x1, waiting for transfers between devices, with_halo(): lax.ppermute(lax.slice_in_dim(block, block.shape[dim] - width, None, axis...  46.4 us
    all_to_all x1, starting transfers between devices, shards(): lax.all_to_all(coeffs, ('range', 'cross'), split_axis=0, concat_axis=0, t...  12 us
    dot_general x1, matrix products, shards(): jnp.dot(source_factor[0], field, preferred_element_type=jnp.float32)  8.49 us
    dot_general x1, matrix products, shards(): far = jnp.dot(target_factor[0], arrived, preferred_element_type=jnp.float32)  7.78 us
    dot_general x1, matrix products, shards(): jnp.dot(target_factor[1], rotate(arrived), preferred_element_type=jnp.flo...  7.23 us
    neg x3, other arithmetic, rotate(): return jnp.concatenate([-block[..., half:], block[..., :half]], axis=-1)  7.04 us
    dot_general x1, matrix products, shards(): jnp.dot(source_factor[1], rotate(field), preferred_element_type=jnp.float32)  6.67 us
    convert_element_type x1, local copies, waits for them, and re-layouts, shards(): coeffs = jnp.where(keep, coeffs, jnp.float32(0.0)).astype(jnp.bfloat16)  6.39 us
  transfers between devices with their start and end apart: 3, of which 2 were waited for; matrix products, arithmetic and copies ran while one was open for 16% of the time, Pallas kernels for 0%

commit v1 on v0

v1 whole, which is shorter than its diff:
```python
import functools

import jax
import jax.numpy as jnp
from jax import lax
from jax.experimental import pallas as pl
from jax.experimental.pallas import tpu as pltpu
from jax.sharding import PartitionSpec as P

RANK = 16
NEAR_B = 128
NB = 3
HALO_BLK = 2
AXES = ("range", "cross")
MIB = 1024 * 1024


def params(mib):
    return pltpu.CompilerParams(vmem_limit_bytes=mib * MIB)


def cost(flops, bytes_accessed):
    return pl.CostEstimate(flops=flops, bytes_accessed=bytes_accessed, transcendentals=0)


def dot(a, b):
    return jnp.dot(a, b, preferred_element_type=jnp.float32)


def coeffs_kernel(rows, depth, count_ref, rank_ref, x_hbm, s_hbm, out_hbm, x_buf, s_buf, held, x_sem, s_sem, out_sem):
    points, cols = x_buf.shape
    half = cols // 2
    tiles = s_buf.shape[1] // rows
    groups = rows // RANK

    def get_x(k):
        place = pl.ds(k * depth, depth)
        return pltpu.make_async_copy(x_hbm.at[place], x_buf.at[place], x_sem.at[k])

    def get_s(tile):
        place = pl.ds(pl.multiple_of(tile * rows, rows), rows)
        return pltpu.make_async_copy(s_hbm.at[:, place], s_buf.at[:, place], s_sem.at[tile])

    def put(tile, slot):
        place = pl.ds(pl.multiple_of(tile * rows, rows), rows)
        return pltpu.make_async_copy(held.at[slot], out_hbm.at[place], out_sem.at[slot])

    def finish(tile, slot, pq):
        place = lax.broadcasted_iota(jnp.int32, (RANK, half), 0)
        for group in range(groups):
            keep = place < rank_ref[tile * groups + group]
            p = pq[group * RANK : (group + 1) * RANK]
            q = pq[rows + group * RANK : rows + (group + 1) * RANK]
            own = slice(group * RANK, (group + 1) * RANK)
            held[slot, own, :half] = jnp.where(keep, p[:, :half] - q[:, half:], 0.0).astype(jnp.bfloat16)
            held[slot, own, half:] = jnp.where(keep, p[:, half:] + q[:, :half], 0.0).astype(jnp.bfloat16)
        put(tile, slot).start()

    parts = points // depth
    get_x(0).start()
    get_s(0).start()
    for k in range(1, parts):
        get_x(k).start()
    for tile in range(1, tiles):
        get_s(tile).start()
    pq = jnp.zeros((2 * rows, cols), jnp.float32)
    get_s_done = False
    for k in range(parts):
        get_x(k).wait()
        own = slice(k * depth, (k + 1) * depth)
        live = lax.broadcasted_iota(jnp.int32, (depth, cols), 0) + k * depth < count_ref[0]
        x = jnp.where(live, x_buf[own].astype(jnp.float32), 0.0).astype(jnp.bfloat16)
        x_buf[own] = x
        if not get_s_done:
            get_s(0).wait()
            get_s_done = True
        pq += dot(s_buf[:, :rows, own].reshape(2 * rows, depth), x)
    finish(0, 0, pq)

    def body(tile, carry):
        slot = lax.rem(tile, 2)
        get_s(tile).wait()
        place = pl.ds(pl.multiple_of(tile * rows, rows), rows)
        full = dot(s_buf[:, place].reshape(2 * rows, points), x_buf[...])

        @pl.when(tile >= 2)
        def _():
            put(tile - 2, slot).wait()

        finish(tile, slot, full)
        return carry

    lax.fori_loop(1, tiles, body, 0)
    for tile in (tiles - 2, tiles - 1):
        put(tile, tile % 2).wait()


def coefficients(count, rank, field, factor, rows=256, depth=256):
    points, cols = field.shape
    total = factor.shape[1]
    return pl.pallas_call(
        functools.partial(coeffs_kernel, rows, depth),
        out_shape=jax.ShapeDtypeStruct((total, cols), jnp.bfloat16),
        in_specs=[pl.BlockSpec(memory_space=pltpu.SMEM)] * 2 + [pl.BlockSpec(memory_space=pl.ANY)] * 2,
        out_specs=pl.BlockSpec(memory_space=pl.ANY),
        scratch_shapes=[
            pltpu.VMEM((points, cols), jnp.bfloat16),
            pltpu.VMEM((2, total, points), jnp.bfloat16),
            pltpu.VMEM((2, rows, cols), jnp.bfloat16),
            pltpu.SemaphoreType.DMA((points // depth,)),
            pltpu.SemaphoreType.DMA((total // rows,)),
            pltpu.SemaphoreType.DMA((2,)),
        ],
        compiler_params=params(60),
        cost_estimate=cost(4 * total * points * cols, 4 * total * points + 2 * (points + total) * cols),
        name="coeffs",
    )(count, rank, field, factor)


def near_kernel(index_ref, count_ref, low_ref, x_ref, high_ref, n_ref, out_ref, window):
    block = pl.program_id(0)
    points, cols = x_ref.shape
    half = cols // 2
    rim = HALO_BLK

    @pl.when(block == 0)
    def _():
        window[:rim] = low_ref[...].reshape(rim, NEAR_B, cols)
        window[rim + points // NEAR_B :] = high_ref[...].reshape(rim, NEAR_B, cols)
        for b in range(points // NEAR_B):
            live = lax.broadcasted_iota(jnp.int32, (NEAR_B, cols), 0) + b * NEAR_B < count_ref[0]
            part = x_ref[b * NEAR_B : (b + 1) * NEAR_B].astype(jnp.float32)
            window[rim + b] = jnp.where(live, part, 0.0).astype(jnp.bfloat16)

    p = jnp.zeros((NEAR_B, cols), jnp.float32)
    q = jnp.zeros((NEAR_B, cols), jnp.float32)
    for k in range(NB):
        x = window[index_ref[block * NB + k]]
        p += dot(n_ref[0, k], x)
        q += dot(n_ref[1, k], x)
    out_ref[:, :half] = p[:, :half] - q[:, half:]
    out_ref[:, half:] = p[:, half:] + q[:, :half]


def near_field(index, count, low, field, high, blocks):
    points, cols = field.shape
    rim = HALO_BLK * NEAR_B
    return pl.pallas_call(
        near_kernel,
        out_shape=jax.ShapeDtypeStruct((points, cols), jnp.float32),
        grid_spec=pltpu.PrefetchScalarGridSpec(
            num_scalar_prefetch=2,
            grid=(points // NEAR_B,),
            in_specs=[
                pl.BlockSpec((rim, cols), lambda i, *_: (0, 0)),
                pl.BlockSpec((points, cols), lambda i, *_: (0, 0)),
                pl.BlockSpec((rim, cols), lambda i, *_: (0, 0)),
                pl.BlockSpec((2, NB, NEAR_B, NEAR_B), lambda i, *_: (0, 0, i, 0)),
            ],
            out_specs=pl.BlockSpec((NEAR_B, cols), lambda i, *_: (i, 0)),
            scratch_shapes=[pltpu.VMEM((points // NEAR_B + 2 * HALO_BLK, NEAR_B, cols), jnp.bfloat16)],
        ),
        compiler_params=params(24),
        cost_estimate=cost(60_000_000_000, 6 * points * cols + 4 * points * NB * NEAR_B),
        name="near",
    )(index, count, low, field, high, blocks)


def far_kernel(rows, part, count_ref, c_hbm, t_hbm, n_hbm, out_hbm, c_buf, t_buf, n_buf, held, c_sem, f_sem, t_sem, n_sem, out_sem):
    depth, cols = c_buf.shape
    points = t_buf.shape[1]
    half = cols // 2
    tiles = points // rows
    parts = depth // part

    def get_c(k):
        place = pl.ds(k * part, part)
        return pltpu.make_async_copy(c_hbm.at[place], c_buf.at[place], c_sem.at[k])

    def get_first(k):
        place = pl.ds(k * part, part)
        return pltpu.make_async_copy(t_hbm.at[:, pl.ds(0, rows), place], t_buf.at[:, pl.ds(0, rows), place], f_sem.at[k])

    def get_t(tile):
        place = pl.ds(tile * rows, rows)
        return pltpu.make_async_copy(t_hbm.at[:, place], t_buf.at[:, place], t_sem.at[tile])

    def get_n(tile):
        place = pl.ds(tile * rows, rows)
        return pltpu.make_async_copy(n_hbm.at[place], n_buf.at[place], n_sem.at[tile])

    def put(tile):
        place = pl.ds(tile * rows, rows)
        return pltpu.make_async_copy(held.at[tile % 2], out_hbm.at[place], out_sem.at[tile % 2])

    def finish(tile, pq):
        get_n(tile).wait()
        if tile >= 2:
            put(tile - 2).wait()
        own = slice(tile * rows, (tile + 1) * rows)
        live = lax.broadcasted_iota(jnp.int32, (rows, half), 0) + tile * rows < count_ref[0]
        real = pq[:rows, :half] - pq[rows:, half:] + n_buf[own, :half]
        imag = pq[:rows, half:] + pq[rows:, :half] + n_buf[own, half:]
        held[tile % 2, :, :half] = jnp.where(live, real, 0.0).astype(jnp.bfloat16)
        held[tile % 2, :, half:] = jnp.where(live, imag, 0.0).astype(jnp.bfloat16)
        put(tile).start()

    for k in range(parts):
        get_c(k).start()
        get_first(k).start()
    get_n(0).start()
    for tile in range(1, tiles):
        get_t(tile).start()
        get_n(tile).start()
    pq = jnp.zeros((2 * rows, cols), jnp.float32)
    for k in range(parts):
        get_c(k).wait()
        get_first(k).wait()
        own = slice(k * part, (k + 1) * part)
        pq += dot(t_buf[:, :rows, own].reshape(2 * rows, part), c_buf[own])
    finish(0, pq)
    for tile in range(1, tiles):
        get_t(tile).wait()
        finish(tile, dot(t_buf[:, tile * rows : (tile + 1) * rows].reshape(2 * rows, depth), c_buf[...]))
    for tile in range(tiles - 2, tiles):
        put(tile).wait()


def far_field(count, arrived, factor, near, rows=256, part=512):
    points, cols = near.shape
    depth = arrived.shape[0]
    return pl.pallas_call(
        functools.partial(far_kernel, rows, part),
        out_shape=jax.ShapeDtypeStruct((points, cols), jnp.bfloat16),
        in_specs=[pl.BlockSpec(memory_space=pltpu.SMEM)] + [pl.BlockSpec(memory_space=pl.ANY)] * 3,
        out_specs=pl.BlockSpec(memory_space=pl.ANY),
        scratch_shapes=[
            pltpu.VMEM((depth, cols), jnp.bfloat16),
            pltpu.VMEM((2, points, depth), jnp.bfloat16),
            pltpu.VMEM((points, cols), jnp.float32),
            pltpu.VMEM((2, rows, cols), jnp.bfloat16),
            pltpu.SemaphoreType.DMA((depth // part,)),
            pltpu.SemaphoreType.DMA((depth // part,)),
            pltpu.SemaphoreType.DMA((points // rows,)),
            pltpu.SemaphoreType.DMA((points // rows,)),
            pltpu.SemaphoreType.DMA((2,)),
        ],
        compiler_params=params(60),
        cost_estimate=cost(4 * points * depth * cols, 4 * points * depth + 2 * depth * cols + 6 * points * cols),
        name="far",
    )(count, arrived, factor, near)


def halo(field, count):
    points = field.shape[0]
    rim = HALO_BLK * NEAR_B
    devices = lax.axis_size("cross")
    forward = [(i, i + 1) for i in range(devices - 1)]
    backward = [(target, source) for source, target in forward]
    rows = lax.broadcasted_iota(jnp.int32, (rim, 1), 0)
    zero = jnp.zeros((), jnp.bfloat16)
    last = jnp.where(rows + (points - rim) < count[0], field[points - rim :], zero)
    return lax.ppermute(last, "cross", forward), lax.ppermute(field[:rim], "cross", backward)


def shards(surface_field, point_count, far_rank, source_factor, target_factor, near_blocks, near_index):
    boxes = far_rank.shape[1]
    cols = surface_field.shape[1]
    low, high = halo(surface_field, point_count)
    coeffs = coefficients(point_count, far_rank.reshape(boxes), surface_field, source_factor)
    coeffs = coeffs.reshape(boxes, RANK, cols)
    arrived = lax.all_to_all(coeffs, AXES, split_axis=0, concat_axis=0, tiled=True)
    near = near_field(
        near_index.reshape(-1), point_count, low, surface_field, high, jnp.transpose(near_blocks, (0, 2, 1, 3))
    )
    return far_field(point_count, arrived.reshape(boxes * RANK, cols), target_factor, near)


def solution(mesh):
    return jax.shard_map(
        shards,
        mesh=mesh,
        in_specs=(
            P(AXES, None),
            P(AXES),
            P(AXES, None),
            P(None, None, AXES),
            P(None, AXES, None),
            P(None, AXES, None, None),
            P(AXES, None),
        ),
        out_specs=P(AXES, None),
        check_vma=False,
    )
```

time: 136 us -> 102 us (0.75)
  matrix products: 34.8 us -> 0 us
  Pallas kernels: 0 us -> 33.7 us
  local copies, waits for them, and re-layouts: 24.2 us -> 3.53 us
  other arithmetic: 10.4 us -> 2.29 us
  waiting for transfers between devices: 48.6 us -> 43.5 us
    ppermute x2, waiting for transfers between devices: 48.6 us -> 0.01 us  [the longest x1 0.01 us: halo(): lax.ppermute(last, 'cross', forward)]
    all_to_all x1, waiting for transfers between devices: 0.01 us -> 43.5 us  [shards(): lax.all_to_all(coeffs, AXES, split_axis=0, concat_axis=0, tiled=True)]
    dot_general x6 -> x0, matrix products: 34.8 us -> none  [the longest x1 8.49 us: shards(): jnp.dot(source_factor[0], field, preferred_element_type=jnp.float32)]
    pallas_call x0 -> x3, Pallas kernels: none -> 33.7 us  [the longest x1 15.2 us: coefficients(): pl.pallas_call(functools.partial(coeffs_kernel, rows, depth), out_shape=j...]
    convert_element_type x2 -> x0, local copies, waits for them, and re-layouts: 8.95 us -> none  [the longest x1 6.39 us: shards(): coeffs = jnp.where(keep, coeffs, jnp.float32(0.0)).astype(jnp.bfloat16)]
    neg x3 -> x0, other arithmetic: 7.04 us -> none  [rotate(): return jnp.concatenate([-block[..., half:], block[..., :half]], axis=-1)]
    reshape x1, local copies, waits for them, and re-layouts: 5.37 us -> 0.08 us  [shards(): near_index.reshape(-1)]
    gather x1 -> x0, local copies, waits for them, and re-layouts: 4.39 us -> none  [shards(): picked = window_blocks[near_index]]
  transfers between devices with their start and end apart: 3 -> 3, of which waited for: 2 -> 1; matrix products, arithmetic and copies ran while one was open for 16% -> 0% of each run, Pallas kernels for 0% -> 21%
where the time goes in v1:
time: 102 us
  waiting for transfers between devices  43.5 us (43%)
  Pallas kernels  33.7 us (33%)
  starting transfers between devices  17.8 us (17%)
  local copies, waits for them, and re-layouts  3.53 us (3%)
  other arithmetic  2.29 us (2%)
    all_to_all x1, waiting for transfers between devices, shards(): lax.all_to_all(coeffs, AXES, split_axis=0, concat_axis=0, tiled=True)  43.5 us
    pallas_call x1, Pallas kernels, coefficients(): pl.pallas_call(functools.partial(coeffs_kernel, rows, depth), out_shape=j...  15.2 us
    pallas_call x1, Pallas kernels, far_field(): pl.pallas_call(functools.partial(far_kernel, rows, part), out_shape=jax.S...  12.7 us
    all_to_all x1, starting transfers between devices, shards(): lax.all_to_all(coeffs, AXES, split_axis=0, concat_axis=0, tiled=True)  12.5 us
    pallas_call x1, Pallas kernels, near_field(): pl.pallas_call(near_kernel, out_shape=jax.ShapeDtypeStruct((points, cols)...  5.76 us
    ppermute x1, starting transfers between devices, halo(): lax.ppermute(last, 'cross', forward)  4.05 us
    unnamed x9, local copies, waits for them, and re-layouts  3.45 us
    slice x1, other arithmetic, halo(): field[:rim]  2.28 us
  transfers between devices with their start and end apart: 3, of which 1 were waited for; matrix products, arithmetic and copies ran while one was open for 0% of the time, Pallas kernels for 21%

profile of v1, /device:TPU:1, one launch (start us, length us, event | category | flops | bytes accessed | tf_op | source)
XLA Modules:
  0.0 101.6 jit_solution(1683926362681314224)
XLA Ops:
  0.7 2.3 %fusion = (bf16[256,1024]{1,0:T(8,128)(2,1)}, bf16[256,1024]{1,0:T(8,128)(2,1)}) fusion(bf16[1024,1024]{1,0:T(8,128)(2,1)} %x_ref.1, pred[256]{0:T(512)(128)(4,1)S(1)} %add_compare_fusion), kind=kLoop, calls=%fused_computation.2 | loop fusion | flops 262144 | bytes 2097408 | tf_op jit(solution)/shard_map/slice | solution.py:263
  3.0 4.1 %collective-permute-start = (bf16[256,1024]{1,0:T(8,128)(2,1)}, bf16[256,1024]{1,0:T(8,128)(2,1)S(1)}, u32[]{:S(2)}, u32[]{:S(2)}) collective-permute-start(bf16[256,1024]{1,0:T(8,128)(2,1)} %get-tuple-element.6), channel_id=1, source_target_pairs={{0,1},{1,2},{2,3},{4,5},{5,6},{6,7},{8,9},{9,10},{10,11},{12,13},{... | collective-permute-start | bytes 1572872 | tf_op jit(solution)/shard_map/ppermute | solution.py:263
  7.0 1.3 %collective-permute-start.1 = (bf16[256,1024]{1,0:T(8,128)(2,1)}, bf16[256,1024]{1,0:T(8,128)(2,1)S(1)}, u32[]{:S(2)}, u32[]{:S(2)}) collective-permute-start(bf16[256,1024]{1,0:T(8,128)(2,1)} %get-tuple-element.5), channel_id=1, source_target_pairs={{1,0},{2,1},{3,2},{5,4},{6,5},{7,6},{9,8},{10,9},{11,10},{13,12},{... | collective-permute-start | bytes 1572872 | tf_op jit(solution)/shard_map/ppermute | solution.py:263
  8.3 15.2 %coeffs.1 = bf16[2048,1024]{1,0:T(8,128)(2,1)} custom-call(s32[1]{0:T(128)} %copy.10.count_ref, s32[128]{0:T(128)} %bitcast.8, bf16[1024,1024]{1,0:T(8,128)(2,1)} %x_ref.1, bf16[2,2048,1024]{2,1,0:T(8,128)(2,1)} %s_hbm.1), custom_call_target="tpu_custom_call" | custom-call | flops 8589934592 | bytes 14680064 | tf_op jit(solution)/shard_map/coeffs/pallas_call | solution.py:101
  23.6 0.0 copy-start.3
  23.6 0.0 copy-start
  23.6 12.5 %all-to-all-start = ((bf16[128,16,1024]{2,1,0:T(8,128)(2,1)}), bf16[128,16,1024]{2,1,0:T(8,128)(2,1)}, u32[]{:S(2)}, u32[]{:S(2)}) async-start(bf16[128,16,1024]{2,1,0:T(8,128)(2,1)} %bitcast.7), calls=%async_computation | async-start | bytes 8388608 | tf_op jit(solution)/shard_map/all_to_all | solution.py:272
  36.0 0.0 copy-done.3
  36.1 0.1 copy.9
  36.1 0.1 reshape.22.index_ref
  36.2 0.0 collective-permute-done.low_ref
  36.2 0.0 collective-permute-done.1.high_ref
  36.2 0.0 copy-done
  36.2 0.0 copy-start.1
  36.3 1.4 %copy-done.1 = bf16[2,1024,3,128]{3,1,2,0:T(8,128)(2,1)S(1)} copy-done((bf16[2,1024,3,128]{3,1,2,0:T(8,128)(2,1)S(1)}, bf16[2,1024,3,128]{3,1,2,0:T(8,128)(2,1)}, u32[]{:S(2)}) %copy-start.1) | copy-done | bytes 1572888
  37.7 5.8 %near.1.n_hbm = f32[1024,1024]{1,0:T(8,128)S(1)} custom-call(s32[24]{0:T(128)S(1)} %reshape.22.index_ref, s32[1]{0:T(128)} %copy.10.count_ref, bf16[256,1024]{1,0:T(8,128)(2,1)S(1)} %collective-permute-done.low_ref, bf16[1024,1024]{1,0:T(8,128)(2,1)S(1)} %copy-done, bf16[256,1024]{1,0:T(8,128)(2,1)S(1)} %collective-permute-done.1.high_ref, ...), custom_call_target="tpu_custom_call" | custom-call | flops 60000002048 | bytes 7864320 | tf_op jit(solution)/shard_map/near/pallas_call | solution.py:148
  43.4 0.0 copy-start.2
  43.4 1.9 %copy-done.2 = f32[1024,1024]{1,0:T(8,128)} copy-done((f32[1024,1024]{1,0:T(8,128)}, f32[1024,1024]{1,0:T(8,128)S(1)}, u32[]{:S(2)}) %copy-start.2) | copy-done | bytes 4194328
  45.4 43.5 %all-to-all-done = bf16[128,16,1024]{2,1,0:T(8,128)(2,1)} async-done(((bf16[128,16,1024]{2,1,0:T(8,128)(2,1)}), bf16[128,16,1024]{2,1,0:T(8,128)(2,1)}, u32[]{:S(2)}, u32[]{:S(2)}) %all-to-all-start) | async-done | bytes 4194336 | tf_op jit(solution)/shard_map/all_to_all | solution.py:272
  88.9 12.7 %far.1 = bf16[1024,1024]{1,0:T(8,128)(2,1)} custom-call(s32[1]{0:T(128)} %copy.10.count_ref, bf16[2048,1024]{1,0:T(8,128)(2,1)} %bitcast.2.c_hbm, bf16[2,1024,2048]{2,1,0:T(8,128)(2,1)} %t_hbm.1, f32[1024,1024]{1,0:T(8,128)} %copy-done.2), custom_call_target="tpu_custom_call" | custom-call | flops 8589934592 | bytes 18874368 | tf_op jit(solution)/shard_map/far/pallas_call | solution.py:232
  (1 shorter events, 0.0 us)
Async XLA Ops:
  3.0 33.3 %collective-permute-start = (bf16[256,1024]{1,0:T(8,128)(2,1)}, bf16[256,1024]{1,0:T(8,128)(2,1)S(1)}, u32[]{:S(2)}, u32[]{:S(2)}) collective-permute-start(bf16[256,1024]{1,0:T(8,128)(2,1)} %get-tuple-element.6), channel_id=1, source_target_pairs={{0,1},{1,2},{2,3},{4,5},{5,6},{6,7},{8,9},{9,10},{10,11},{12,13},{... | collective-permute-start | bytes 1572872 | tf_op jit(solution)/shard_map/ppermute | solution.py:263
  7.0 29.2 %collective-permute-start.1 = (bf16[256,1024]{1,0:T(8,128)(2,1)}, bf16[256,1024]{1,0:T(8,128)(2,1)S(1)}, u32[]{:S(2)}, u32[]{:S(2)}) collective-permute-start(bf16[256,1024]{1,0:T(8,128)(2,1)} %get-tuple-element.5), channel_id=1, source_target_pairs={{1,0},{2,1},{3,2},{5,4},{6,5},{7,6},{9,8},{10,9},{11,10},{13,12},{... | collective-permute-start | bytes 1572872 | tf_op jit(solution)/shard_map/ppermute | solution.py:263
  23.6 12.5 %copy-start.3 = (s32[8,3]{0,1:T(4,128)S(1)}, s32[8,3]{0,1:T(4,128)}, u32[]{:S(2)}) copy-start(s32[8,3]{0,1:T(4,128)} %param.13) | copy-start | bytes 292
  23.6 12.7 %copy-start = (bf16[1024,1024]{1,0:T(8,128)(2,1)S(1)}, bf16[1024,1024]{1,0:T(8,128)(2,1)}, u32[]{:S(2)}) copy-start(bf16[1024,1024]{1,0:T(8,128)(2,1)} %x_ref.1) | copy-start | bytes 6291460
  23.6 65.3 %all-to-all-start = ((bf16[128,16,1024]{2,1,0:T(8,128)(2,1)}), bf16[128,16,1024]{2,1,0:T(8,128)(2,1)}, u32[]{:S(2)}, u32[]{:S(2)}) async-start(bf16[128,16,1024]{2,1,0:T(8,128)(2,1)} %bitcast.7), calls=%async_computation | async-start | bytes 8388608 | tf_op jit(solution)/shard_map/all_to_all | solution.py:272
  36.2 1.4 %copy-start.1 = (bf16[2,1024,3,128]{3,1,2,0:T(8,128)(2,1)S(1)}, bf16[2,1024,3,128]{3,1,2,0:T(8,128)(2,1)}, u32[]{:S(2)}) copy-start(bf16[2,1024,3,128]{3,1,2,0:T(8,128)(2,1)} %param.12) | copy-start | bytes 4718596
  43.4 2.0 %copy-start.2 = (f32[1024,1024]{1,0:T(8,128)}, f32[1024,1024]{1,0:T(8,128)S(1)}, u32[]{:S(2)}) copy-start(f32[1024,1024]{1,0:T(8,128)S(1)} %near.1.n_hbm) | copy-start | bytes 12582916

commit v2 on v1

v2 whole, which is shorter than its diff:
```python
import functools

import jax
import jax.numpy as jnp
from jax import lax
from jax.experimental import pallas as pl
from jax.experimental.pallas import tpu as pltpu
from jax.sharding import PartitionSpec as P

RANK = 16
NEAR_B = 128
NB = 3
HALO_BLK = 2
AXES = ("range", "cross")
MIB = 1024 * 1024


def params(mib):
    return pltpu.CompilerParams(vmem_limit_bytes=mib * MIB)


def cost(flops, bytes_accessed):
    return pl.CostEstimate(flops=flops, bytes_accessed=bytes_accessed, transcendentals=0)


def dot(a, b):
    return jnp.dot(a, b, preferred_element_type=jnp.float32)


def coeffs_kernel(
    tiles, depth, count_ref, rank_ref, x_hbm, s_hbm, out_hbm, low_hbm, high_hbm,
    x_buf, s_buf, held, x_sem, s_sem, out_sem, edge_sem
):
    points, cols = x_hbm.shape
    width = cols // 2
    parts = points // depth
    rim = low_hbm.shape[0]
    first = 0
    edges = (
        pltpu.make_async_copy(x_buf.at[pl.ds(0, rim)], low_hbm, edge_sem.at[0]),
        pltpu.make_async_copy(x_buf.at[pl.ds(points - rim, rim)], high_hbm, edge_sem.at[1]),
    )

    def rows_of(tile):
        return sum(tiles[:tile]), tiles[tile]

    def get_x(k, side):
        place = pl.ds(k * depth, depth)
        there = pl.ds(first + side * (cols // 2), width)
        return pltpu.make_async_copy(
            x_hbm.at[place, there], x_buf.at[place, pl.ds(side * width, width)], x_sem.at[k, side]
        )

    def get_s(tile):
        place = pl.ds(*rows_of(tile))
        return pltpu.make_async_copy(s_hbm.at[:, place], s_buf.at[:, place], s_sem.at[tile])

    def put(tile):
        place = pl.ds(*rows_of(tile))
        return pltpu.make_async_copy(held.at[place], out_hbm.at[place], out_sem.at[tile])

    def finish(tile, total):
        start, rows = rows_of(tile)
        place = lax.broadcasted_iota(jnp.int32, (RANK, 2 * width), 0)
        for group in range(rows // RANK):
            keep = place < rank_ref[start // RANK + group]
            part = total[group * RANK : (group + 1) * RANK]
            held[start + group * RANK : start + (group + 1) * RANK] = jnp.where(keep, part, 0.0).astype(jnp.bfloat16)
        put(tile).start()

    for k in range(min(parts, 2)):
        get_x(k, 0).start()
        get_x(k, 1).start()
        if k == 0:
            get_s(0).start()
    total = jnp.zeros((tiles[0], 2 * width), jnp.float32)
    for k in range(parts):
        get_x(k, 0).wait()
        get_x(k, 1).wait()
        own = slice(k * depth, (k + 1) * depth)
        turned = slice(points + k * depth, points + (k + 1) * depth)
        x = x_buf[own]
        if 2 * k * depth >= points:
            live = lax.broadcasted_iota(jnp.int32, x.shape, 0) + k * depth < count_ref[0]
            x = jnp.where(live, x.astype(jnp.float32), 0.0).astype(jnp.bfloat16)
            x_buf[own] = x
        x_buf[turned, :width] = -x[:, width:]
        x_buf[turned, width:] = x[:, :width]
        if k == 0:
            get_s(0).wait()
        if k + 2 < parts:
            get_x(k + 2, 0).start()
            get_x(k + 2, 1).start()
        if k == parts - 2:
            get_s(1).start()
        total += dot(s_buf[0, : tiles[0], own], x_buf[own]) + dot(s_buf[1, : tiles[0], own], x_buf[turned])
    finish(0, total)
    for edge in edges:
        edge.start()
    for tile in range(1, len(tiles)):
        start, rows = rows_of(tile)
        get_s(tile).wait()
        if tile + 1 < len(tiles):
            get_s(tile + 1).start()
        own = slice(start, start + rows)
        finish(tile, dot(jnp.concatenate([s_buf[0, own], s_buf[1, own]], axis=1), x_buf[...]))
    for edge in edges:
        edge.wait()
    for tile in range(len(tiles)):
        put(tile).wait()


def coefficients(count, rank, field, factor, depth=512, tiles=(256, 512, 1024, 256)):
    points, cols = field.shape
    total = factor.shape[1]
    width = cols // 2
    edge = jax.ShapeDtypeStruct((HALO_BLK * NEAR_B, cols), jnp.bfloat16)
    return pl.pallas_call(
        functools.partial(coeffs_kernel, tiles, depth),
        out_shape=[jax.ShapeDtypeStruct((total, cols), jnp.bfloat16), edge, edge],
        in_specs=[pl.BlockSpec(memory_space=pltpu.SMEM)] * 2 + [pl.BlockSpec(memory_space=pl.ANY)] * 2,
        out_specs=[pl.BlockSpec(memory_space=pl.ANY)] * 3,
        scratch_shapes=[
            pltpu.VMEM((2 * points, 2 * width), jnp.bfloat16),
            pltpu.VMEM((2, total, points), jnp.bfloat16),
            pltpu.VMEM((total, 2 * width), jnp.bfloat16),
            pltpu.SemaphoreType.DMA((points // depth, 2)),
            pltpu.SemaphoreType.DMA((len(tiles),)),
            pltpu.SemaphoreType.DMA((len(tiles),)),
            pltpu.SemaphoreType.DMA((2,)),
        ],
        compiler_params=params(60),
        cost_estimate=cost(8 * total * points * width, 4 * total * points + 4 * (points + total) * width),
        name="coeffs",
    )(count, rank, field, factor)


def near_kernel(index_ref, count_ref, low_ref, x_ref, high_ref, n_ref, out_ref, window):
    block = pl.program_id(0)
    points, cols = x_ref.shape
    half = cols // 2
    rim = HALO_BLK

    @pl.when(block == 0)
    def _():
        window[:rim] = low_ref[...].reshape(rim, NEAR_B, cols)
        window[rim + points // NEAR_B :] = high_ref[...].reshape(rim, NEAR_B, cols)
        for b in range(points // NEAR_B):
            live = lax.broadcasted_iota(jnp.int32, (NEAR_B, cols), 0) + b * NEAR_B < count_ref[0]
            part = x_ref[b * NEAR_B : (b + 1) * NEAR_B].astype(jnp.float32)
            window[rim + b] = jnp.where(live, part, 0.0).astype(jnp.bfloat16)

    p = jnp.zeros((NEAR_B, cols), jnp.float32)
    q = jnp.zeros((NEAR_B, cols), jnp.float32)
    for k in range(NB):
        x = window[index_ref[block * NB + k]]
        p += dot(n_ref[0, k], x)
        q += dot(n_ref[1, k], x)
    out_ref[:, :half] = p[:, :half] - q[:, half:]
    out_ref[:, half:] = p[:, half:] + q[:, :half]


def near_field(index, count, low, field, high, blocks):
    points, cols = field.shape
    rim = HALO_BLK * NEAR_B
    return pl.pallas_call(
        near_kernel,
        out_shape=jax.ShapeDtypeStruct((points, cols), jnp.float32),
        grid_spec=pltpu.PrefetchScalarGridSpec(
            num_scalar_prefetch=2,
            grid=(points // NEAR_B,),
            in_specs=[
                pl.BlockSpec((rim, cols), lambda i, *_: (0, 0)),
                pl.BlockSpec((points, cols), lambda i, *_: (0, 0)),
                pl.BlockSpec((rim, cols), lambda i, *_: (0, 0)),
                pl.BlockSpec((2, NB, NEAR_B, NEAR_B), lambda i, *_: (0, 0, i, 0)),
            ],
            out_specs=pl.BlockSpec((NEAR_B, cols), lambda i, *_: (i, 0)),
            scratch_shapes=[pltpu.VMEM((points // NEAR_B + 2 * HALO_BLK, NEAR_B, cols), jnp.bfloat16)],
        ),
        compiler_params=params(24),
        cost_estimate=cost(60_000_000_000, 6 * points * cols + 4 * points * NB * NEAR_B),
        name="near",
    )(index, count, low, field, high, blocks)


def far_kernel(first, tiles, part, count_ref, c_hbm, t_hbm, n_hbm, *refs):
    out_hbm, c_buf, t_buf, n_buf, held, c_sem, f_sem, t_sem, n_sem, out_sem = refs[-10:]
    depth = c_hbm.shape[0]
    cols = n_hbm.shape[1]
    width = c_hbm.shape[1] // 2
    parts = depth // part

    def rows_of(tile):
        return sum(tiles[:tile]), tiles[tile]

    def get_c(k):
        place = pl.ds(k * part, part)
        return pltpu.make_async_copy(c_hbm.at[place], c_buf.at[place], c_sem.at[k])

    def get_first(k):
        rows, place = pl.ds(0, tiles[0]), pl.ds(k * part, part)
        return pltpu.make_async_copy(t_hbm.at[:, rows, place], t_buf.at[:, rows, place], f_sem.at[k])

    def get_t(tile):
        place = pl.ds(*rows_of(tile))
        return pltpu.make_async_copy(t_hbm.at[:, place], t_buf.at[:, place], t_sem.at[tile])

    def get_n(tile, side):
        place = pl.ds(*rows_of(tile))
        there, here = pl.ds(first + side * (cols // 2), width), pl.ds(side * width, width)
        return pltpu.make_async_copy(n_hbm.at[place, there], n_buf.at[place, here], n_sem.at[tile, side])

    def put(tile, side):
        place = pl.ds(*rows_of(tile))
        there, here = pl.ds(first + side * (cols // 2), width), pl.ds(side * width, width)
        return pltpu.make_async_copy(held.at[place, here], out_hbm.at[place, there], out_sem.at[tile, side])

    def finish(tile, pq):
        start, rows = rows_of(tile)
        get_n(tile, 0).wait()
        get_n(tile, 1).wait()
        own = slice(start, start + rows)
        live = lax.broadcasted_iota(jnp.int32, (rows, width), 0) + start < count_ref[0]
        real = pq[:rows, :width] - pq[rows:, width:] + n_buf[own, :width]
        imag = pq[:rows, width:] + pq[rows:, :width] + n_buf[own, width:]
        held[own, :width] = jnp.where(live, real, 0.0).astype(jnp.bfloat16)
        held[own, width:] = jnp.where(live, imag, 0.0).astype(jnp.bfloat16)
        put(tile, 0).start()
        put(tile, 1).start()

    def get_more(tile):
        get_t(tile).start()
        get_n(tile, 0).start()
        get_n(tile, 1).start()

    for k in range(min(parts, 2)):
        get_c(k).start()
        get_first(k).start()
    pq = jnp.zeros((2 * tiles[0], 2 * width), jnp.float32)
    for k in range(parts):
        get_c(k).wait()
        get_first(k).wait()
        if k + 2 < parts:
            get_c(k + 2).start()
            get_first(k + 2).start()
        if k == parts - 2:
            get_n(0, 0).start()
            get_n(0, 1).start()
            get_more(1)
        own = slice(k * part, (k + 1) * part)
        pq += dot(t_buf[:, : tiles[0], own].reshape(2 * tiles[0], part), c_buf[own])
    finish(0, pq)
    for tile in range(1, len(tiles)):
        start, rows = rows_of(tile)
        get_t(tile).wait()
        if tile + 1 < len(tiles):
            get_more(tile + 1)
        finish(tile, dot(t_buf[:, start : start + rows].reshape(2 * rows, depth), c_buf[...]))
    for tile in range(len(tiles)):
        put(tile, 0).wait()
        put(tile, 1).wait()


def far_field(first, count, arrived, factor, near, out, part=512, tiles=(256, 512, 256)):
    points, cols = near.shape
    depth, wide = arrived.shape
    kept = [] if out is None else [out]
    return pl.pallas_call(
        functools.partial(far_kernel, first, tiles, part),
        out_shape=jax.ShapeDtypeStruct((points, cols), jnp.bfloat16),
        in_specs=[pl.BlockSpec(memory_space=pltpu.SMEM)] + [pl.BlockSpec(memory_space=pl.ANY)] * (3 + len(kept)),
        out_specs=pl.BlockSpec(memory_space=pl.ANY),
        scratch_shapes=[
            pltpu.VMEM((depth, wide), jnp.bfloat16),
            pltpu.VMEM((2, points, depth), jnp.bfloat16),
            pltpu.VMEM((points, wide), jnp.float32),
            pltpu.VMEM((points, wide), jnp.bfloat16),
            pltpu.SemaphoreType.DMA((depth // part,)),
            pltpu.SemaphoreType.DMA((depth // part,)),
            pltpu.SemaphoreType.DMA((len(tiles),)),
            pltpu.SemaphoreType.DMA((len(tiles), 2)),
            pltpu.SemaphoreType.DMA((len(tiles), 2)),
        ],
        input_output_aliases={4: 0} if kept else {},
        compiler_params=params(60),
        cost_estimate=cost(4 * points * depth * wide, 4 * points * depth + 2 * depth * wide + 6 * points * wide),
        name=f"far_{first}",
    )(count, arrived, factor, near, *kept)


def halo(first, last):
    devices = lax.axis_size("cross")
    forward = [(i, i + 1) for i in range(devices - 1)]
    backward = [(target, source) for source, target in forward]
    return lax.ppermute(last, "cross", forward), lax.ppermute(first, "cross", backward)


def shards(surface_field, point_count, far_rank, source_factor, target_factor, near_blocks, near_index):
    boxes = far_rank.shape[1]
    cols = surface_field.shape[1]
    coeffs, first, last = coefficients(point_count, far_rank.reshape(boxes), surface_field, source_factor)
    low, high = halo(first, last)
    arrived = lax.all_to_all(coeffs.reshape(boxes, RANK, cols), AXES, split_axis=0, concat_axis=0, tiled=True)
    near = near_field(
        near_index.reshape(-1), point_count, low, surface_field, high, jnp.transpose(near_blocks, (0, 2, 1, 3))
    )
    return far_field(0, point_count, arrived.reshape(boxes * RANK, cols), target_factor, near, None)


def solution(mesh):
    return jax.shard_map(
        shards,
        mesh=mesh,
        in_specs=(
            P(AXES, None),
            P(AXES),
            P(AXES, None),
            P(None, None, AXES),
            P(None, AXES, None),
            P(None, AXES, None, None),
            P(AXES, None),
        ),
        out_specs=P(AXES, None),
        check_vma=False,
    )
```

time: 102 us -> 98.6 us (0.967)
  other arithmetic: 2.29 us -> 0 us
  Pallas kernels: 33.7 us -> 32.6 us
    slice x1 -> x0, other arithmetic: 2.28 us -> none  [halo(): field[:rim]]
    pallas_call x2, Pallas kernels: 28 us -> 26.8 us  [the longest x1 13.8 us: far_field(): pl.pallas_call(functools.partial(far_kernel, first, tiles, part), out_sha...]
  transfers between devices with their start and end apart: 3 -> 3, of which waited for: 1 -> 2; matrix products, arithmetic and copies ran while one was open for 0% -> 0% of each run, Pallas kernels for 21% -> 6%
where the time goes in v2:
time: 98.6 us; the launch traced here: 98.4 us
  waiting for transfers between devices  43.6 us (44%)
  Pallas kernels  32.6 us (33%)
  starting transfers between devices  17.8 us (18%)
  local copies, waits for them, and re-layouts  3.54 us (4%)
    all_to_all x1, waiting for transfers between devices, shards(): lax.all_to_all(coeffs.reshape(boxes, RANK, cols), AXES, split_axis=0, con...  42.9 us
    pallas_call x1, Pallas kernels, far_field(): pl.pallas_call(functools.partial(far_kernel, first, tiles, part), out_sha...  13.8 us
    pallas_call x1, Pallas kernels, coefficients(): pl.pallas_call(functools.partial(coeffs_kernel, tiles, depth), out_shape=...  13 us
    all_to_all x1, starting transfers between devices, shards(): lax.all_to_all(coeffs.reshape(boxes, RANK, cols), AXES, split_axis=0, con...  12.5 us
    pallas_call x1, Pallas kernels, near_field(): pl.pallas_call(near_kernel, out_shape=jax.ShapeDtypeStruct((points, cols)...  5.73 us
    ppermute x1, starting transfers between devices, halo(): lax.ppermute(last, 'cross', forward)  4.06 us
    unnamed x9, local copies, waits for them, and re-layouts  3.45 us
  transfers between devices with their start and end apart: 3, of which 2 were waited for; matrix products, arithmetic and copies ran while one was open for 0% of the time, Pallas kernels for 6%

profile of v2, /device:TPU:1, one launch (start us, length us, event | category | flops | bytes accessed | tf_op | source)
XLA Modules:
  0.0 98.4 jit_solution(3291118112048340963)
XLA Ops:
  0.7 13.0 %coeffs.1 = (bf16[2048,1024]{1,0:T(8,128)(2,1)}, bf16[256,1024]{1,0:T(8,128)(2,1)}, bf16[256,1024]{1,0:T(8,128)(2,1)}) custom-call(s32[1]{0:T(128)S(6)} %copy.10.count_ref, s32[128]{0:T(128)} %bitcast.6, bf16[1024,1024]{1,0:T(8,128)(2,1)} %x_ref.1, bf16[2,2048,1024]{2,1,0:T(8,128)(2,1)} %s_hbm.1), custom_call_target="tpu_custom_call" | custom-call | flops 8589934592 | bytes 14680064 | tf_op jit(solution)/shard_map/coeffs/pallas_call | solution.py:118
  13.7 4.1 %collective-permute-start = (bf16[256,1024]{1,0:T(8,128)(2,1)}, bf16[256,1024]{1,0:T(8,128)(2,1)S(1)}, u32[]{:S(2)}, u32[]{:S(2)}) collective-permute-start(bf16[256,1024]{1,0:T(8,128)(2,1)} %get-tuple-element.9), channel_id=1, source_target_pairs={{0,1},{1,2},{2,3},{4,5},{5,6},{6,7},{8,9},{9,10},{10,11},{12,13},{... | collective-permute-start | bytes 1572872 | tf_op jit(solution)/shard_map/ppermute | solution.py:296
  17.8 1.3 %collective-permute-start.1 = (bf16[256,1024]{1,0:T(8,128)(2,1)}, bf16[256,1024]{1,0:T(8,128)(2,1)S(1)}, u32[]{:S(2)}, u32[]{:S(2)}) collective-permute-start(bf16[256,1024]{1,0:T(8,128)(2,1)} %get-tuple-element.10), channel_id=1, source_target_pairs={{1,0},{2,1},{3,2},{5,4},{6,5},{7,6},{9,8},{10,9},{11,10},{13,12},{... | collective-permute-start | bytes 1572872 | tf_op jit(solution)/shard_map/ppermute | solution.py:296
  19.1 0.0 copy-start.3
  19.1 0.0 copy-start
  19.1 12.5 %all-to-all-start = ((bf16[128,16,1024]{2,1,0:T(8,128)(2,1)}), bf16[128,16,1024]{2,1,0:T(8,128)(2,1)}, u32[]{:S(2)}, u32[]{:S(2)}) async-start(bf16[128,16,1024]{2,1,0:T(8,128)(2,1)} %bitcast.5), calls=%async_computation | async-start | bytes 8388608 | tf_op jit(solution)/shard_map/all_to_all | solution.py:304
  31.6 0.0 copy-done.3
  31.6 0.1 copy.9
  31.7 0.1 reshape.15.index_ref
  31.7 0.0 collective-permute-done.low_ref
  31.7 0.6 collective-permute-done.1.high_ref
  32.3 0.0 copy-done
  32.3 0.0 copy-start.1
  32.3 1.4 %copy-done.1 = bf16[2,1024,3,128]{3,1,2,0:T(8,128)(2,1)S(1)} copy-done((bf16[2,1024,3,128]{3,1,2,0:T(8,128)(2,1)S(1)}, bf16[2,1024,3,128]{3,1,2,0:T(8,128)(2,1)}, u32[]{:S(2)}) %copy-start.1) | copy-done | bytes 1572888
  33.8 5.7 %near.1.n_hbm = f32[1024,1024]{1,0:T(8,128)S(1)} custom-call(s32[24]{0:T(128)S(1)} %reshape.15.index_ref, s32[1]{0:T(128)S(6)} %copy.10.count_ref, bf16[256,1024]{1,0:T(8,128)(2,1)S(1)} %collective-permute-done.low_ref, bf16[1024,1024]{1,0:T(8,128)(2,1)S(1)} %copy-done, bf16[256,1024]{1,0:T(8,128)(2,1)S(1)} %collective-permute-done.1.high_ref, ...), custom_call_target="tpu_custom_call" | custom-call | flops 60000002048 | bytes 7864320 | tf_op jit(solution)/shard_map/near/pallas_call | solution.py:166
  39.5 0.0 copy-start.2
  39.5 1.9 %copy-done.2 = f32[1024,1024]{1,0:T(8,128)} copy-done((f32[1024,1024]{1,0:T(8,128)}, f32[1024,1024]{1,0:T(8,128)S(1)}, u32[]{:S(2)}) %copy-start.2) | copy-done | bytes 4194328
  41.5 42.9 %all-to-all-done = bf16[128,16,1024]{2,1,0:T(8,128)(2,1)} async-done(((bf16[128,16,1024]{2,1,0:T(8,128)(2,1)}), bf16[128,16,1024]{2,1,0:T(8,128)(2,1)}, u32[]{:S(2)}, u32[]{:S(2)}) %all-to-all-start) | async-done | bytes 4194336 | tf_op jit(solution)/shard_map/all_to_all | solution.py:304
  84.4 13.8 %far_0.1 = bf16[1024,1024]{1,0:T(8,128)(2,1)} custom-call(s32[1]{0:T(128)S(6)} %copy.10.count_ref, bf16[2048,1024]{1,0:T(8,128)(2,1)} %bitcast.2.c_hbm, bf16[2,1024,2048]{2,1,0:T(8,128)(2,1)} %t_hbm.1, f32[1024,1024]{1,0:T(8,128)} %copy-done.2), custom_call_target="tpu_custom_call" | custom-call | flops 8589934592 | bytes 18874368 | tf_op jit(solution)/shard_map/far_0/pallas_call | solution.py:269
Async XLA Ops:
  13.7 18.0 %collective-permute-start = (bf16[256,1024]{1,0:T(8,128)(2,1)}, bf16[256,1024]{1,0:T(8,128)(2,1)S(1)}, u32[]{:S(2)}, u32[]{:S(2)}) collective-permute-start(bf16[256,1024]{1,0:T(8,128)(2,1)} %get-tuple-element.9), channel_id=1, source_target_pairs={{0,1},{1,2},{2,3},{4,5},{5,6},{6,7},{8,9},{9,10},{10,11},{12,13},{... | collective-permute-start | bytes 1572872 | tf_op jit(solution)/shard_map/ppermute | solution.py:296
  17.8 14.6 %collective-permute-start.1 = (bf16[256,1024]{1,0:T(8,128)(2,1)}, bf16[256,1024]{1,0:T(8,128)(2,1)S(1)}, u32[]{:S(2)}, u32[]{:S(2)}) collective-permute-start(bf16[256,1024]{1,0:T(8,128)(2,1)} %get-tuple-element.10), channel_id=1, source_target_pairs={{1,0},{2,1},{3,2},{5,4},{6,5},{7,6},{9,8},{10,9},{11,10},{13,12},{... | collective-permute-start | bytes 1572872 | tf_op jit(solution)/shard_map/ppermute | solution.py:296
  19.1 12.5 %copy-start.3 = (s32[8,3]{0,1:T(4,128)S(1)}, s32[8,3]{0,1:T(4,128)}, u32[]{:S(2)}) copy-start(s32[8,3]{0,1:T(4,128)} %param.13) | copy-start | bytes 292
  19.1 13.3 %copy-start = (bf16[1024,1024]{1,0:T(8,128)(2,1)S(1)}, bf16[1024,1024]{1,0:T(8,128)(2,1)}, u32[]{:S(2)}) copy-start(bf16[1024,1024]{1,0:T(8,128)(2,1)} %x_ref.1) | copy-start | bytes 6291460
  19.1 65.3 %all-to-all-start = ((bf16[128,16,1024]{2,1,0:T(8,128)(2,1)}), bf16[128,16,1024]{2,1,0:T(8,128)(2,1)}, u32[]{:S(2)}, u32[]{:S(2)}) async-start(bf16[128,16,1024]{2,1,0:T(8,128)(2,1)} %bitcast.5), calls=%async_computation | async-start | bytes 8388608 | tf_op jit(solution)/shard_map/all_to_all | solution.py:304
  32.3 1.4 %copy-start.1 = (bf16[2,1024,3,128]{3,1,2,0:T(8,128)(2,1)S(1)}, bf16[2,1024,3,128]{3,1,2,0:T(8,128)(2,1)}, u32[]{:S(2)}) copy-start(bf16[2,1024,3,128]{3,1,2,0:T(8,128)(2,1)} %param.12) | copy-start | bytes 4718596
  39.5 2.0 %copy-start.2 = (f32[1024,1024]{1,0:T(8,128)}, f32[1024,1024]{1,0:T(8,128)S(1)}, u32[]{:S(2)}) copy-start(f32[1024,1024]{1,0:T(8,128)S(1)} %near.1.n_hbm) | copy-start | bytes 12582916

commit v3 on v2

--- a/solution.py
+++ b/solution.py
@@ -184,11 +184,11 @@
     )(index, count, low, field, high, blocks)
 
 
-def far_kernel(first, tiles, part, count_ref, c_hbm, t_hbm, n_hbm, *refs):
-    out_hbm, c_buf, t_buf, n_buf, held, c_sem, f_sem, t_sem, n_sem, out_sem = refs[-10:]
-    depth = c_hbm.shape[0]
-    cols = n_hbm.shape[1]
-    width = c_hbm.shape[1] // 2
+def far_kernel(
+    tiles, part, count_ref, c_hbm, t_hbm, n_hbm, out_hbm, c_buf, t_buf, n_buf, held, c_sem, f_sem, t_sem, n_sem, out_sem
+):
+    depth, cols = c_hbm.shape
+    half = cols // 2
     parts = depth // part
 
     def rows_of(tile):
@@ -206,87 +206,70 @@
         place = pl.ds(*rows_of(tile))
         return pltpu.make_async_copy(t_hbm.at[:, place], t_buf.at[:, place], t_sem.at[tile])
 
-    def get_n(tile, side):
-        place = pl.ds(*rows_of(tile))
-        there, here = pl.ds(first + side * (cols // 2), width), pl.ds(side * width, width)
-        return pltpu.make_async_copy(n_hbm.at[place, there], n_buf.at[place, here], n_sem.at[tile, side])
-
-    def put(tile, side):
-        place = pl.ds(*rows_of(tile))
-        there, here = pl.ds(first + side * (cols // 2), width), pl.ds(side * width, width)
-        return pltpu.make_async_copy(held.at[place, here], out_hbm.at[place, there], out_sem.at[tile, side])
+    def get_n(tile):
+        place = pl.ds(*rows_of(tile))
+        return pltpu.make_async_copy(n_hbm.at[place], n_buf.at[place], n_sem.at[tile])
+
+    def put(tile):
+        place = pl.ds(*rows_of(tile))
+        return pltpu.make_async_copy(held.at[place], out_hbm.at[place], out_sem.at[tile])
 
     def finish(tile, pq):
-        start, rows = rows_of(tile)
-        get_n(tile, 0).wait()
-        get_n(tile, 1).wait()
-        own = slice(start, start + rows)
-        live = lax.broadcasted_iota(jnp.int32, (rows, width), 0) + start < count_ref[0]
-        real = pq[:rows, :width] - pq[rows:, width:] + n_buf[own, :width]
-        imag = pq[:rows, width:] + pq[rows:, :width] + n_buf[own, width:]
-        held[own, :width] = jnp.where(live, real, 0.0).astype(jnp.bfloat16)
-        held[own, width:] = jnp.where(live, imag, 0.0).astype(jnp.bfloat16)
-        put(tile, 0).start()
-        put(tile, 1).start()
-
-    def get_more(tile):
-        get_t(tile).start()
-        get_n(tile, 0).start()
-        get_n(tile, 1).start()
-
-    for k in range(min(parts, 2)):
+        first, rows = rows_of(tile)
+        get_n(tile).wait()
+        own = slice(first, first + rows)
+        live = lax.broadcasted_iota(jnp.int32, (rows, half), 0) + first < count_ref[0]
+        real = pq[:rows, :half] - pq[rows:, half:] + n_buf[own, :half]
+        imag = pq[:rows, half:] + pq[rows:, :half] + n_buf[own, half:]
+        held[own, :half] = jnp.where(live, real, 0.0).astype(jnp.bfloat16)
+        held[own, half:] = jnp.where(live, imag, 0.0).astype(jnp.bfloat16)
+        put(tile).start()
+
+    for k in range(parts):
         get_c(k).start()
         get_first(k).start()
-    pq = jnp.zeros((2 * tiles[0], 2 * width), jnp.float32)
+    get_n(0).start()
+    for tile in range(1, len(tiles)):
+        get_t(tile).start()
+        get_n(tile).start()
+    pq = jnp.zeros((2 * tiles[0], cols), jnp.float32)
     for k in range(parts):
         get_c(k).wait()
         get_first(k).wait()
-        if k + 2 < parts:
-            get_c(k + 2).start()
-            get_first(k + 2).start()
-        if k == parts - 2:
-            get_n(0, 0).start()
-            get_n(0, 1).start()
-            get_more(1)
         own = slice(k * part, (k + 1) * part)
         pq += dot(t_buf[:, : tiles[0], own].reshape(2 * tiles[0], part), c_buf[own])
     finish(0, pq)
     for tile in range(1, len(tiles)):
-        start, rows = rows_of(tile)
+        first, rows = rows_of(tile)
         get_t(tile).wait()
-        if tile + 1 < len(tiles):
-            get_more(tile + 1)
-        finish(tile, dot(t_buf[:, start : start + rows].reshape(2 * rows, depth), c_buf[...]))
+        finish(tile, dot(t_buf[:, first : first + rows].reshape(2 * rows, depth), c_buf[...]))
     for tile in range(len(tiles)):
-        put(tile, 0).wait()
-        put(tile, 1).wait()
-
-
-def far_field(first, count, arrived, factor, near, out, part=512, tiles=(256, 512, 256)):
+        put(tile).wait()
+
+
+def far_field(count, arrived, factor, near, part=512, tiles=(256, 512, 256)):
     points, cols = near.shape
-    depth, wide = arrived.shape
-    kept = [] if out is None else [out]
+    depth = arrived.shape[0]
     return pl.pallas_call(
-        functools.partial(far_kernel, first, tiles, part),
+        functools.partial(far_kernel, tiles, part),
         out_shape=jax.ShapeDtypeStruct((points, cols), jnp.bfloat16),
-        in_specs=[pl.BlockSpec(memory_space=pltpu.SMEM)] + [pl.BlockSpec(memory_space=pl.ANY)] * (3 + len(kept)),
+        in_specs=[pl.BlockSpec(memory_space=pltpu.SMEM)] + [pl.BlockSpec(memory_space=pl.ANY)] * 3,
         out_specs=pl.BlockSpec(memory_space=pl.ANY),
         scratch_shapes=[
-            pltpu.VMEM((depth, wide), jnp.bfloat16),
+            pltpu.VMEM((depth, cols), jnp.bfloat16),
             pltpu.VMEM((2, points, depth), jnp.bfloat16),
-            pltpu.VMEM((points, wide), jnp.float32),
-            pltpu.VMEM((points, wide), jnp.bfloat16),
+            pltpu.VMEM((points, cols), jnp.float32),
+            pltpu.VMEM((points, cols), jnp.bfloat16),
             pltpu.SemaphoreType.DMA((depth // part,)),
             pltpu.SemaphoreType.DMA((depth // part,)),
             pltpu.SemaphoreType.DMA((len(tiles),)),
-            pltpu.SemaphoreType.DMA((len(tiles), 2)),
-            pltpu.SemaphoreType.DMA((len(tiles), 2)),
+            pltpu.SemaphoreType.DMA((len(tiles),)),
+            pltpu.SemaphoreType.DMA((len(tiles),)),
         ],
-        input_output_aliases={4: 0} if kept else {},
         compiler_params=params(60),
-        cost_estimate=cost(4 * points * depth * wide, 4 * points * depth + 2 * depth * wide + 6 * points * wide),
-        name=f"far_{first}",
-    )(count, arrived, factor, near, *kept)
+        cost_estimate=cost(4 * points * depth * cols, 4 * points * depth + 2 * depth * cols + 6 * points * cols),
+        name="far",
+    )(count, arrived, factor, near)
 
 
 def halo(first, last):
@@ -305,7 +288,7 @@
     near = near_field(
         near_index.reshape(-1), point_count, low, surface_field, high, jnp.transpose(near_blocks, (0, 2, 1, 3))
     )
-    return far_field(0, point_count, arrived.reshape(boxes * RANK, cols), target_factor, near, None)
+    return far_field(point_count, arrived.reshape(boxes * RANK, cols), target_factor, near)
 
 
 def solution(mesh):

time: 98.6 us -> 97.4 us (0.988)
  Pallas kernels: 32.6 us -> 31.3 us
    pallas_call x1, Pallas kernels: 13.8 us -> 12.5 us  [far_field(): pl.pallas_call(functools.partial(far_kernel, tiles, part), out_shape=jax....]
where the time goes in v3:
time: 97.4 us; the launch traced here: 97.1 us
  waiting for transfers between devices  43.6 us (45%)
  Pallas kernels  31.3 us (32%)
  starting transfers between devices  17.8 us (18%)
  local copies, waits for them, and re-layouts  3.54 us (4%)
    all_to_all x1, waiting for transfers between devices, shards(): lax.all_to_all(coeffs.reshape(boxes, RANK, cols), AXES, split_axis=0, con...  42.9 us
    pallas_call x1, Pallas kernels, coefficients(): pl.pallas_call(functools.partial(coeffs_kernel, tiles, depth), out_shape=...  13 us
    pallas_call x1, Pallas kernels, far_field(): pl.pallas_call(functools.partial(far_kernel, tiles, part), out_shape=jax....  12.5 us
    all_to_all x1, starting transfers between devices, shards(): lax.all_to_all(coeffs.reshape(boxes, RANK, cols), AXES, split_axis=0, con...  12.5 us
    pallas_call x1, Pallas kernels, near_field(): pl.pallas_call(near_kernel, out_shape=jax.ShapeDtypeStruct((points, cols)...  5.73 us
    ppermute x1, starting transfers between devices, halo(): lax.ppermute(last, 'cross', forward)  4.06 us
    unnamed x9, local copies, waits for them, and re-layouts  3.45 us
  transfers between devices with their start and end apart: 3, of which 2 were waited for; matrix products, arithmetic and copies ran while one was open for 0% of the time, Pallas kernels for 6%

profile of v3, /device:TPU:1, one launch (start us, length us, event | category | flops | bytes accessed | tf_op | source)
XLA Modules:
  0.0 97.1 jit_solution(15901531402525615435)
XLA Ops:
  0.7 13.0 %coeffs.1 = (bf16[2048,1024]{1,0:T(8,128)(2,1)}, bf16[256,1024]{1,0:T(8,128)(2,1)}, bf16[256,1024]{1,0:T(8,128)(2,1)}) custom-call(s32[1]{0:T(128)S(6)} %copy.10.count_ref, s32[128]{0:T(128)} %bitcast.6, bf16[1024,1024]{1,0:T(8,128)(2,1)} %x_ref.1, bf16[2,2048,1024]{2,1,0:T(8,128)(2,1)} %s_hbm.1), custom_call_target="tpu_custom_call" | custom-call | flops 8589934592 | bytes 14680064 | tf_op jit(solution)/shard_map/coeffs/pallas_call | solution.py:118
  13.7 4.1 %collective-permute-start = (bf16[256,1024]{1,0:T(8,128)(2,1)}, bf16[256,1024]{1,0:T(8,128)(2,1)S(1)}, u32[]{:S(2)}, u32[]{:S(2)}) collective-permute-start(bf16[256,1024]{1,0:T(8,128)(2,1)} %get-tuple-element.9), channel_id=1, source_target_pairs={{0,1},{1,2},{2,3},{4,5},{5,6},{6,7},{8,9},{9,10},{10,11},{12,13},{... | collective-permute-start | bytes 1572872 | tf_op jit(solution)/shard_map/ppermute | solution.py:279
  17.8 1.3 %collective-permute-start.1 = (bf16[256,1024]{1,0:T(8,128)(2,1)}, bf16[256,1024]{1,0:T(8,128)(2,1)S(1)}, u32[]{:S(2)}, u32[]{:S(2)}) collective-permute-start(bf16[256,1024]{1,0:T(8,128)(2,1)} %get-tuple-element.10), channel_id=1, source_target_pairs={{1,0},{2,1},{3,2},{5,4},{6,5},{7,6},{9,8},{10,9},{11,10},{13,12},{... | collective-permute-start | bytes 1572872 | tf_op jit(solution)/shard_map/ppermute | solution.py:279
  19.1 0.0 copy-start.3
  19.1 0.0 copy-start
  19.1 12.5 %all-to-all-start = ((bf16[128,16,1024]{2,1,0:T(8,128)(2,1)}), bf16[128,16,1024]{2,1,0:T(8,128)(2,1)}, u32[]{:S(2)}, u32[]{:S(2)}) async-start(bf16[128,16,1024]{2,1,0:T(8,128)(2,1)} %bitcast.5), calls=%async_computation | async-start | bytes 8388608 | tf_op jit(solution)/shard_map/all_to_all | solution.py:287
  31.6 0.0 copy-done.3
  31.6 0.1 copy.9
  31.7 0.1 reshape.15.index_ref
  31.7 0.0 collective-permute-done.low_ref
  31.7 0.6 collective-permute-done.1.high_ref
  32.3 0.0 copy-done
  32.3 0.0 copy-start.1
  32.3 1.4 %copy-done.1 = bf16[2,1024,3,128]{3,1,2,0:T(8,128)(2,1)S(1)} copy-done((bf16[2,1024,3,128]{3,1,2,0:T(8,128)(2,1)S(1)}, bf16[2,1024,3,128]{3,1,2,0:T(8,128)(2,1)}, u32[]{:S(2)}) %copy-start.1) | copy-done | bytes 1572888
  33.8 5.7 %near.1.n_hbm = f32[1024,1024]{1,0:T(8,128)S(1)} custom-call(s32[24]{0:T(128)S(1)} %reshape.15.index_ref, s32[1]{0:T(128)S(6)} %copy.10.count_ref, bf16[256,1024]{1,0:T(8,128)(2,1)S(1)} %collective-permute-done.low_ref, bf16[1024,1024]{1,0:T(8,128)(2,1)S(1)} %copy-done, bf16[256,1024]{1,0:T(8,128)(2,1)S(1)} %collective-permute-done.1.high_ref, ...), custom_call_target="tpu_custom_call" | custom-call | flops 60000002048 | bytes 7864320 | tf_op jit(solution)/shard_map/near/pallas_call | solution.py:166
  39.5 0.0 copy-start.2
  39.5 1.9 %copy-done.2 = f32[1024,1024]{1,0:T(8,128)} copy-done((f32[1024,1024]{1,0:T(8,128)}, f32[1024,1024]{1,0:T(8,128)S(1)}, u32[]{:S(2)}) %copy-start.2) | copy-done | bytes 4194328
  41.5 42.9 %all-to-all-done = bf16[128,16,1024]{2,1,0:T(8,128)(2,1)} async-done(((bf16[128,16,1024]{2,1,0:T(8,128)(2,1)}), bf16[128,16,1024]{2,1,0:T(8,128)(2,1)}, u32[]{:S(2)}, u32[]{:S(2)}) %all-to-all-start) | async-done | bytes 4194336 | tf_op jit(solution)/shard_map/all_to_all | solution.py:287
  84.4 12.5 %far.1 = bf16[1024,1024]{1,0:T(8,128)(2,1)} custom-call(s32[1]{0:T(128)S(6)} %copy.10.count_ref, bf16[2048,1024]{1,0:T(8,128)(2,1)} %bitcast.2.c_hbm, bf16[2,1024,2048]{2,1,0:T(8,128)(2,1)} %t_hbm.1, f32[1024,1024]{1,0:T(8,128)} %copy-done.2), custom_call_target="tpu_custom_call" | custom-call | flops 8589934592 | bytes 18874368 | tf_op jit(solution)/shard_map/far/pallas_call | solution.py:253
Async XLA Ops:
  13.7 18.0 %collective-permute-start = (bf16[256,1024]{1,0:T(8,128)(2,1)}, bf16[256,1024]{1,0:T(8,128)(2,1)S(1)}, u32[]{:S(2)}, u32[]{:S(2)}) collective-permute-start(bf16[256,1024]{1,0:T(8,128)(2,1)} %get-tuple-element.9), channel_id=1, source_target_pairs={{0,1},{1,2},{2,3},{4,5},{5,6},{6,7},{8,9},{9,10},{10,11},{12,13},{... | collective-permute-start | bytes 1572872 | tf_op jit(solution)/shard_map/ppermute | solution.py:279
  17.8 14.6 %collective-permute-start.1 = (bf16[256,1024]{1,0:T(8,128)(2,1)}, bf16[256,1024]{1,0:T(8,128)(2,1)S(1)}, u32[]{:S(2)}, u32[]{:S(2)}) collective-permute-start(bf16[256,1024]{1,0:T(8,128)(2,1)} %get-tuple-element.10), channel_id=1, source_target_pairs={{1,0},{2,1},{3,2},{5,4},{6,5},{7,6},{9,8},{10,9},{11,10},{13,12},{... | collective-permute-start | bytes 1572872 | tf_op jit(solution)/shard_map/ppermute | solution.py:279
  19.1 12.5 %copy-start.3 = (s32[8,3]{0,1:T(4,128)S(1)}, s32[8,3]{0,1:T(4,128)}, u32[]{:S(2)}) copy-start(s32[8,3]{0,1:T(4,128)} %param.13) | copy-start | bytes 292
  19.1 13.3 %copy-start = (bf16[1024,1024]{1,0:T(8,128)(2,1)S(1)}, bf16[1024,1024]{1,0:T(8,128)(2,1)}, u32[]{:S(2)}) copy-start(bf16[1024,1024]{1,0:T(8,128)(2,1)} %x_ref.1) | copy-start | bytes 6291460
  19.1 65.3 %all-to-all-start = ((bf16[128,16,1024]{2,1,0:T(8,128)(2,1)}), bf16[128,16,1024]{2,1,0:T(8,128)(2,1)}, u32[]{:S(2)}, u32[]{:S(2)}) async-start(bf16[128,16,1024]{2,1,0:T(8,128)(2,1)} %bitcast.5), calls=%async_computation | async-start | bytes 8388608 | tf_op jit(solution)/shard_map/all_to_all | solution.py:287
  32.3 1.4 %copy-start.1 = (bf16[2,1024,3,128]{3,1,2,0:T(8,128)(2,1)S(1)}, bf16[2,1024,3,128]{3,1,2,0:T(8,128)(2,1)}, u32[]{:S(2)}) copy-start(bf16[2,1024,3,128]{3,1,2,0:T(8,128)(2,1)} %param.12) | copy-start | bytes 4718596
  39.5 2.0 %copy-start.2 = (f32[1024,1024]{1,0:T(8,128)}, f32[1024,1024]{1,0:T(8,128)S(1)}, u32[]{:S(2)}) copy-start(f32[1024,1024]{1,0:T(8,128)S(1)} %near.1.n_hbm) | copy-start | bytes 12582916

commit v4 on v3

--- a/solution.py
+++ b/solution.py
@@ -156,8 +156,8 @@
         x = window[index_ref[block * NB + k]]
         p += dot(n_ref[0, k], x)
         q += dot(n_ref[1, k], x)
-    out_ref[:, :half] = p[:, :half] - q[:, half:]
-    out_ref[:, half:] = p[:, half:] + q[:, :half]
+    out_ref[:, :half] = (p[:, :half] - q[:, half:]).astype(out_ref.dtype)
+    out_ref[:, half:] = (p[:, half:] + q[:, :half]).astype(out_ref.dtype)
 
 
 def near_field(index, count, low, field, high, blocks):
@@ -165,7 +165,7 @@
     rim = HALO_BLK * NEAR_B
     return pl.pallas_call(
         near_kernel,
-        out_shape=jax.ShapeDtypeStruct((points, cols), jnp.float32),
+        out_shape=jax.ShapeDtypeStruct((points, cols), jnp.bfloat16),
         grid_spec=pltpu.PrefetchScalarGridSpec(
             num_scalar_prefetch=2,
             grid=(points // NEAR_B,),
@@ -219,8 +219,8 @@
         get_n(tile).wait()
         own = slice(first, first + rows)
         live = lax.broadcasted_iota(jnp.int32, (rows, half), 0) + first < count_ref[0]
-        real = pq[:rows, :half] - pq[rows:, half:] + n_buf[own, :half]
-        imag = pq[:rows, half:] + pq[rows:, :half] + n_buf[own, half:]
+        real = pq[:rows, :half] - pq[rows:, half:] + n_buf[own, :half].astype(jnp.float32)
+        imag = pq[:rows, half:] + pq[rows:, :half] + n_buf[own, half:].astype(jnp.float32)
         held[own, :half] = jnp.where(live, real, 0.0).astype(jnp.bfloat16)
         held[own, half:] = jnp.where(live, imag, 0.0).astype(jnp.bfloat16)
         put(tile).start()
@@ -258,7 +258,7 @@
         scratch_shapes=[
             pltpu.VMEM((depth, cols), jnp.bfloat16),
             pltpu.VMEM((2, points, depth), jnp.bfloat16),
-            pltpu.VMEM((points, cols), jnp.float32),
+            pltpu.VMEM((points, cols), jnp.bfloat16),
             pltpu.VMEM((points, cols), jnp.bfloat16),
             pltpu.SemaphoreType.DMA((depth // part,)),
             pltpu.SemaphoreType.DMA((depth // part,)),

time: 97.4 us -> 97.5 us (level)
  no operation moved by 1% of the time
where the time goes in v4:
time: 97.5 us; the launch traced here: 97.2 us
  waiting for transfers between devices  44.1 us (45%)
  Pallas kernels  31.4 us (32%)
  starting transfers between devices  17.8 us (18%)
  local copies, waits for them, and re-layouts  2.94 us (3%)
    all_to_all x1, waiting for transfers between devices, shards(): lax.all_to_all(coeffs.reshape(boxes, RANK, cols), AXES, split_axis=0, con...  43.5 us
    pallas_call x1, Pallas kernels, coefficients(): pl.pallas_call(functools.partial(coeffs_kernel, tiles, depth), out_shape=...  13 us
    pallas_call x1, Pallas kernels, far_field(): pl.pallas_call(functools.partial(far_kernel, tiles, part), out_shape=jax....  12.7 us
    all_to_all x1, starting transfers between devices, shards(): lax.all_to_all(coeffs.reshape(boxes, RANK, cols), AXES, split_axis=0, con...  12.5 us
    pallas_call x1, Pallas kernels, near_field(): pl.pallas_call(near_kernel, out_shape=jax.ShapeDtypeStruct((points, cols)...  5.74 us
    ppermute x1, starting transfers between devices, halo(): lax.ppermute(last, 'cross', forward)  4.06 us
    unnamed x9, local copies, waits for them, and re-layouts  2.86 us
  transfers between devices with their start and end apart: 3, of which 2 were waited for; matrix products, arithmetic and copies ran while one was open for 0% of the time, Pallas kernels for 6%

profile of v4, /device:TPU:1, one launch (start us, length us, event | category | flops | bytes accessed | tf_op | source)
XLA Modules:
  0.0 97.2 jit_solution(8131209204707392567)
XLA Ops:
  0.7 13.0 %coeffs.1 = (bf16[2048,1024]{1,0:T(8,128)(2,1)}, bf16[256,1024]{1,0:T(8,128)(2,1)}, bf16[256,1024]{1,0:T(8,128)(2,1)}) custom-call(s32[1]{0:T(128)S(6)} %copy.10.count_ref, s32[128]{0:T(128)} %bitcast.6, bf16[1024,1024]{1,0:T(8,128)(2,1)} %x_ref.1, bf16[2,2048,1024]{2,1,0:T(8,128)(2,1)} %s_hbm.1), custom_call_target="tpu_custom_call" | custom-call | flops 8589934592 | bytes 14680064 | tf_op jit(solution)/shard_map/coeffs/pallas_call | solution.py:118
  13.7 4.1 %collective-permute-start = (bf16[256,1024]{1,0:T(8,128)(2,1)}, bf16[256,1024]{1,0:T(8,128)(2,1)S(1)}, u32[]{:S(2)}, u32[]{:S(2)}) collective-permute-start(bf16[256,1024]{1,0:T(8,128)(2,1)} %get-tuple-element.9), channel_id=1, source_target_pairs={{0,1},{1,2},{2,3},{4,5},{5,6},{6,7},{8,9},{9,10},{10,11},{12,13},{... | collective-permute-start | bytes 1572872 | tf_op jit(solution)/shard_map/ppermute | solution.py:279
  17.8 1.3 %collective-permute-start.1 = (bf16[256,1024]{1,0:T(8,128)(2,1)}, bf16[256,1024]{1,0:T(8,128)(2,1)S(1)}, u32[]{:S(2)}, u32[]{:S(2)}) collective-permute-start(bf16[256,1024]{1,0:T(8,128)(2,1)} %get-tuple-element.10), channel_id=1, source_target_pairs={{1,0},{2,1},{3,2},{5,4},{6,5},{7,6},{9,8},{10,9},{11,10},{13,12},{... | collective-permute-start | bytes 1572872 | tf_op jit(solution)/shard_map/ppermute | solution.py:279
  19.1 0.0 copy-start.3
  19.1 0.0 copy-start
  19.1 12.5 %all-to-all-start = ((bf16[128,16,1024]{2,1,0:T(8,128)(2,1)}), bf16[128,16,1024]{2,1,0:T(8,128)(2,1)}, u32[]{:S(2)}, u32[]{:S(2)}) async-start(bf16[128,16,1024]{2,1,0:T(8,128)(2,1)} %bitcast.5), calls=%async_computation | async-start | bytes 8388608 | tf_op jit(solution)/shard_map/all_to_all | solution.py:287
  31.6 0.0 copy-done.3
  31.6 0.1 copy.9
  31.7 0.1 reshape.15.index_ref
  31.7 0.0 collective-permute-done.low_ref
  31.7 0.6 collective-permute-done.1.high_ref
  32.3 0.0 copy-done
  32.3 0.0 copy-start.1
  32.3 1.4 %copy-done.1 = bf16[2,1024,3,128]{3,1,2,0:T(8,128)(2,1)S(1)} copy-done((bf16[2,1024,3,128]{3,1,2,0:T(8,128)(2,1)S(1)}, bf16[2,1024,3,128]{3,1,2,0:T(8,128)(2,1)}, u32[]{:S(2)}) %copy-start.1) | copy-done | bytes 1572888
  33.8 5.7 %near.1.n_hbm = bf16[1024,1024]{1,0:T(8,128)(2,1)S(1)} custom-call(s32[24]{0:T(128)S(1)} %reshape.15.index_ref, s32[1]{0:T(128)S(6)} %copy.10.count_ref, bf16[256,1024]{1,0:T(8,128)(2,1)S(1)} %collective-permute-done.low_ref, bf16[1024,1024]{1,0:T(8,128)(2,1)S(1)} %copy-done, bf16[256,1024]{1,0:T(8,128)(2,1)S(1)} %collective-permute-done.1.high_ref, ...), custom_call_target="tpu_custom_call" | custom-call | flops 60000002048 | bytes 7864320 | tf_op jit(solution)/shard_map/near/pallas_call | solution.py:166
  39.5 0.0 copy-start.2
  39.5 1.4 %copy-done.2 = bf16[1024,1024]{1,0:T(8,128)(2,1)} copy-done((bf16[1024,1024]{1,0:T(8,128)(2,1)}, bf16[1024,1024]{1,0:T(8,128)(2,1)S(1)}, u32[]{:S(2)}) %copy-start.2) | copy-done | bytes 2097176
  40.9 43.5 %all-to-all-done = bf16[128,16,1024]{2,1,0:T(8,128)(2,1)} async-done(((bf16[128,16,1024]{2,1,0:T(8,128)(2,1)}), bf16[128,16,1024]{2,1,0:T(8,128)(2,1)}, u32[]{:S(2)}, u32[]{:S(2)}) %all-to-all-start) | async-done | bytes 4194336 | tf_op jit(solution)/shard_map/all_to_all | solution.py:287
  84.4 12.7 %far.1 = bf16[1024,1024]{1,0:T(8,128)(2,1)} custom-call(s32[1]{0:T(128)S(6)} %copy.10.count_ref, bf16[2048,1024]{1,0:T(8,128)(2,1)} %bitcast.2.c_hbm, bf16[2,1024,2048]{2,1,0:T(8,128)(2,1)} %t_hbm.1, bf16[1024,1024]{1,0:T(8,128)(2,1)} %copy-done.2), custom_call_target="tpu_custom_call" | custom-call | flops 8589934592 | bytes 18874368 | tf_op jit(solution)/shard_map/far/pallas_call | solution.py:253
Async XLA Ops:
  13.7 18.0 %collective-permute-start = (bf16[256,1024]{1,0:T(8,128)(2,1)}, bf16[256,1024]{1,0:T(8,128)(2,1)S(1)}, u32[]{:S(2)}, u32[]{:S(2)}) collective-permute-start(bf16[256,1024]{1,0:T(8,128)(2,1)} %get-tuple-element.9), channel_id=1, source_target_pairs={{0,1},{1,2},{2,3},{4,5},{5,6},{6,7},{8,9},{9,10},{10,11},{12,13},{... | collective-permute-start | bytes 1572872 | tf_op jit(solution)/shard_map/ppermute | solution.py:279
  17.8 14.6 %collective-permute-start.1 = (bf16[256,1024]{1,0:T(8,128)(2,1)}, bf16[256,1024]{1,0:T(8,128)(2,1)S(1)}, u32[]{:S(2)}, u32[]{:S(2)}) collective-permute-start(bf16[256,1024]{1,0:T(8,128)(2,1)} %get-tuple-element.10), channel_id=1, source_target_pairs={{1,0},{2,1},{3,2},{5,4},{6,5},{7,6},{9,8},{10,9},{11,10},{13,12},{... | collective-permute-start | bytes 1572872 | tf_op jit(solution)/shard_map/ppermute | solution.py:279
  19.1 12.5 %copy-start.3 = (s32[8,3]{0,1:T(4,128)S(1)}, s32[8,3]{0,1:T(4,128)}, u32[]{:S(2)}) copy-start(s32[8,3]{0,1:T(4,128)} %param.13) | copy-start | bytes 292
  19.1 13.3 %copy-start = (bf16[1024,1024]{1,0:T(8,128)(2,1)S(1)}, bf16[1024,1024]{1,0:T(8,128)(2,1)}, u32[]{:S(2)}) copy-start(bf16[1024,1024]{1,0:T(8,128)(2,1)} %x_ref.1) | copy-start | bytes 6291460
  19.1 65.3 %all-to-all-start = ((bf16[128,16,1024]{2,1,0:T(8,128)(2,1)}), bf16[128,16,1024]{2,1,0:T(8,128)(2,1)}, u32[]{:S(2)}, u32[]{:S(2)}) async-start(bf16[128,16,1024]{2,1,0:T(8,128)(2,1)} %bitcast.5), calls=%async_computation | async-start | bytes 8388608 | tf_op jit(solution)/shard_map/all_to_all | solution.py:287
  32.3 1.4 %copy-start.1 = (bf16[2,1024,3,128]{3,1,2,0:T(8,128)(2,1)S(1)}, bf16[2,1024,3,128]{3,1,2,0:T(8,128)(2,1)}, u32[]{:S(2)}) copy-start(bf16[2,1024,3,128]{3,1,2,0:T(8,128)(2,1)} %param.12) | copy-start | bytes 4718596
  39.5 1.4 %copy-start.2 = (bf16[1024,1024]{1,0:T(8,128)(2,1)}, bf16[1024,1024]{1,0:T(8,128)(2,1)S(1)}, u32[]{:S(2)}) copy-start(bf16[1024,1024]{1,0:T(8,128)(2,1)S(1)} %near.1.n_hbm) | copy-start | bytes 6291460

commit v5 on v3

--- a/solution.py
+++ b/solution.py
@@ -36,9 +36,11 @@
     parts = points // depth
     rim = low_hbm.shape[0]
     first = 0
+    odd = lax.rem(lax.axis_index("cross"), 2)
+    inner, outer = (1 - odd) * (points - rim), odd * (points - rim)
     edges = (
-        pltpu.make_async_copy(x_buf.at[pl.ds(0, rim)], low_hbm, edge_sem.at[0]),
-        pltpu.make_async_copy(x_buf.at[pl.ds(points - rim, rim)], high_hbm, edge_sem.at[1]),
+        pltpu.make_async_copy(x_buf.at[pl.ds(pl.multiple_of(inner, rim), rim)], low_hbm, edge_sem.at[0]),
+        pltpu.make_async_copy(x_buf.at[pl.ds(pl.multiple_of(outer, rim), rim)], high_hbm, edge_sem.at[1]),
     )
 
     def rows_of(tile):
@@ -272,11 +274,13 @@
     )(count, arrived, factor, near)
 
 
-def halo(first, last):
+def halo(inner, outer):
     devices = lax.axis_size("cross")
-    forward = [(i, i + 1) for i in range(devices - 1)]
-    backward = [(target, source) for source, target in forward]
-    return lax.ppermute(last, "cross", forward), lax.ppermute(first, "cross", backward)
+    pairs = [[(i, i + 1) for i in range(start, devices - 1, 2)] for start in (0, 1)]
+    swaps = [one + [(b, a) for a, b in one] for one in pairs]
+    inner, outer = lax.ppermute(inner, "cross", swaps[0]), lax.ppermute(outer, "cross", swaps[1])
+    even = lax.rem(lax.axis_index("cross"), 2) == 0
+    return jnp.where(even, outer, inner), jnp.where(even, inner, outer)
 
 
 def shards(surface_field, point_count, far_rank, source_factor, target_factor, near_blocks, near_index):

time: 97.4 us -> 94.5 us (0.970)
  starting transfers between devices: 17.8 us -> 15 us
    all_to_all x1, starting transfers between devices: 12.5 us -> 9.56 us  [shards(): lax.all_to_all(coeffs.reshape(boxes, RANK, cols), AXES, split_axis=0, con...]
    all_to_all x1, waiting for transfers between devices: 42.9 us -> 41.7 us  [shards(): lax.all_to_all(coeffs.reshape(boxes, RANK, cols), AXES, split_axis=0, con...]
    ppermute x2, waiting for transfers between devices: 0.61 us -> 1.79 us  [the longest x1 1.79 us: halo(): lax.ppermute(inner, 'cross', swaps[0])]
where the time goes in v5:
time: 94.5 us; the launch traced here: 94.2 us
  waiting for transfers between devices  43.5 us (46%)
  Pallas kernels  31.3 us (33%)
  starting transfers between devices  15 us (16%)
  local copies, waits for them, and re-layouts  3.54 us (4%)
    all_to_all x1, waiting for transfers between devices, shards(): lax.all_to_all(coeffs.reshape(boxes, RANK, cols), AXES, split_axis=0, con...  41.7 us
    pallas_call x1, Pallas kernels, coefficients(): pl.pallas_call(functools.partial(coeffs_kernel, tiles, depth), out_shape=...  13 us
    pallas_call x1, Pallas kernels, far_field(): pl.pallas_call(functools.partial(far_kernel, tiles, part), out_shape=jax....  12.5 us
    all_to_all x1, starting transfers between devices, shards(): lax.all_to_all(coeffs.reshape(boxes, RANK, cols), AXES, split_axis=0, con...  9.56 us
    pallas_call x1, Pallas kernels, near_field(): pl.pallas_call(near_kernel, out_shape=jax.ShapeDtypeStruct((points, cols)...  5.72 us
    ppermute x1, starting transfers between devices, halo(): lax.ppermute(inner, 'cross', swaps[0])  4.72 us
    unnamed x9, local copies, waits for them, and re-layouts  3.46 us
  transfers between devices with their start and end apart: 3, of which 2 were waited for; matrix products, arithmetic and copies ran while one was open for 0% of the time, Pallas kernels for 6%

profile of v5, /device:TPU:1, one launch (start us, length us, event | category | flops | bytes accessed | tf_op | source)
XLA Modules:
  0.0 94.2 jit_solution(5143959969500545529)
XLA Ops:
  0.7 13.0 %coeffs.1 = (bf16[2048,1024]{1,0:T(8,128)(2,1)}, bf16[256,1024]{1,0:T(8,128)(2,1)}, bf16[256,1024]{1,0:T(8,128)(2,1)}) custom-call(s32[1]{0:T(128)S(6)} %copy.10.count_ref, s32[128]{0:T(128)} %bitcast.6, bf16[1024,1024]{1,0:T(8,128)(2,1)} %x_ref.1, bf16[2,2048,1024]{2,1,0:T(8,128)(2,1)} %s_hbm.1), custom_call_target="tpu_custom_call" | custom-call | flops 8589934592 | bytes 14680064 | tf_op jit(solution)/shard_map/coeffs/pallas_call | solution.py:120
  13.7 0.7 collective-permute-start
  14.4 4.7 %collective-permute-start.1 = (bf16[256,1024]{1,0:T(8,128)(2,1)}, bf16[256,1024]{1,0:T(8,128)(2,1)S(1)}, u32[]{:S(2)}, u32[]{:S(2)}) collective-permute-start(bf16[256,1024]{1,0:T(8,128)(2,1)} %get-tuple-element.10), channel_id=1, source_target_pairs={{0,1},{2,3},{1,0},{3,2},{4,5},{6,7},{5,4},{7,6},{8,9},{10,11},{9,8... | collective-permute-start | bytes 1572872 | tf_op jit(solution)/shard_map/ppermute | solution.py:281
  19.1 0.0 copy-start.3
  19.1 0.0 copy-start
  19.1 9.6 %all-to-all-start = ((bf16[128,16,1024]{2,1,0:T(8,128)(2,1)}), bf16[128,16,1024]{2,1,0:T(8,128)(2,1)}, u32[]{:S(2)}, u32[]{:S(2)}) async-start(bf16[128,16,1024]{2,1,0:T(8,128)(2,1)} %bitcast.5), calls=%async_computation | async-start | bytes 8388608 | tf_op jit(solution)/shard_map/all_to_all | solution.py:291
  28.7 0.0 copy-done.3
  28.7 0.1 copy.9
  28.8 0.1 reshape.15.index_ref
  28.9 0.0 collective-permute-done
  28.9 1.8 %collective-permute-done.1 = bf16[256,1024]{1,0:T(8,128)(2,1)S(1)} collective-permute-done((bf16[256,1024]{1,0:T(8,128)(2,1)}, bf16[256,1024]{1,0:T(8,128)(2,1)S(1)}, u32[]{:S(2)}, u32[]{:S(2)}) %collective-permute-start.1) | collective-permute-done | bytes 524320 | tf_op jit(solution)/shard_map/ppermute | solution.py:281
  30.6 0.1 broadcast_select_fusion
  30.7 0.0 copy-done
  30.7 0.0 copy-start.1
  30.7 1.4 %copy-done.1 = bf16[2,1024,3,128]{3,1,2,0:T(8,128)(2,1)S(1)} copy-done((bf16[2,1024,3,128]{3,1,2,0:T(8,128)(2,1)S(1)}, bf16[2,1024,3,128]{3,1,2,0:T(8,128)(2,1)}, u32[]{:S(2)}) %copy-start.1) | copy-done | bytes 1572888
  32.1 5.7 %near.1.n_hbm = f32[1024,1024]{1,0:T(8,128)S(1)} custom-call(s32[24]{0:T(128)S(1)} %reshape.15.index_ref, s32[1]{0:T(128)S(6)} %copy.10.count_ref, bf16[256,1024]{1,0:T(8,128)(2,1)S(1)} %get-tuple-element.12.low_ref, bf16[1024,1024]{1,0:T(8,128)(2,1)S(1)} %copy-done, bf16[256,1024]{1,0:T(8,128)(2,1)S(1)} %get-tuple-element.11.high_ref, ...), custom_call_target="tpu_custom_call" | custom-call | flops 60000002048 | bytes 7864320 | tf_op jit(solution)/shard_map/near/pallas_call | solution.py:168
  37.9 0.0 copy-start.2
  37.9 2.0 %copy-done.2 = f32[1024,1024]{1,0:T(8,128)} copy-done((f32[1024,1024]{1,0:T(8,128)}, f32[1024,1024]{1,0:T(8,128)S(1)}, u32[]{:S(2)}) %copy-start.2) | copy-done | bytes 4194328
  39.8 41.7 %all-to-all-done = bf16[128,16,1024]{2,1,0:T(8,128)(2,1)} async-done(((bf16[128,16,1024]{2,1,0:T(8,128)(2,1)}), bf16[128,16,1024]{2,1,0:T(8,128)(2,1)}, u32[]{:S(2)}, u32[]{:S(2)}) %all-to-all-start) | async-done | bytes 4194336 | tf_op jit(solution)/shard_map/all_to_all | solution.py:291
  81.5 12.5 %far.1 = bf16[1024,1024]{1,0:T(8,128)(2,1)} custom-call(s32[1]{0:T(128)S(6)} %copy.10.count_ref, bf16[2048,1024]{1,0:T(8,128)(2,1)} %bitcast.2.c_hbm, bf16[2,1024,2048]{2,1,0:T(8,128)(2,1)} %t_hbm.1, f32[1024,1024]{1,0:T(8,128)} %copy-done.2), custom_call_target="tpu_custom_call" | custom-call | flops 8589934592 | bytes 18874368 | tf_op jit(solution)/shard_map/far/pallas_call | solution.py:255
Async XLA Ops:
  13.7 15.2 %collective-permute-start = (bf16[256,1024]{1,0:T(8,128)(2,1)}, bf16[256,1024]{1,0:T(8,128)(2,1)S(1)}, u32[]{:S(2)}, u32[]{:S(2)}) collective-permute-start(bf16[256,1024]{1,0:T(8,128)(2,1)} %get-tuple-element.9), channel_id=1, source_target_pairs={{1,2},{2,1},{5,6},{6,5},{9,10},{10,9},{13,14},{14,13},{17,18},{18,... | collective-permute-start | bytes 1572872 | tf_op jit(solution)/shard_map/ppermute | solution.py:281
  14.4 16.3 %collective-permute-start.1 = (bf16[256,1024]{1,0:T(8,128)(2,1)}, bf16[256,1024]{1,0:T(8,128)(2,1)S(1)}, u32[]{:S(2)}, u32[]{:S(2)}) collective-permute-start(bf16[256,1024]{1,0:T(8,128)(2,1)} %get-tuple-element.10), channel_id=1, source_target_pairs={{0,1},{2,3},{1,0},{3,2},{4,5},{6,7},{5,4},{7,6},{8,9},{10,11},{9,8... | collective-permute-start | bytes 1572872 | tf_op jit(solution)/shard_map/ppermute | solution.py:281
  19.1 9.6 %copy-start.3 = (s32[8,3]{0,1:T(4,128)S(1)}, s32[8,3]{0,1:T(4,128)}, u32[]{:S(2)}) copy-start(s32[8,3]{0,1:T(4,128)} %param.13) | copy-start | bytes 292
  19.1 11.6 %copy-start = (bf16[1024,1024]{1,0:T(8,128)(2,1)S(1)}, bf16[1024,1024]{1,0:T(8,128)(2,1)}, u32[]{:S(2)}) copy-start(bf16[1024,1024]{1,0:T(8,128)(2,1)} %x_ref.1) | copy-start | bytes 6291460
  19.1 62.4 %all-to-all-start = ((bf16[128,16,1024]{2,1,0:T(8,128)(2,1)}), bf16[128,16,1024]{2,1,0:T(8,128)(2,1)}, u32[]{:S(2)}, u32[]{:S(2)}) async-start(bf16[128,16,1024]{2,1,0:T(8,128)(2,1)} %bitcast.5), calls=%async_computation | async-start | bytes 8388608 | tf_op jit(solution)/shard_map/all_to_all | solution.py:291
  30.7 1.4 %copy-start.1 = (bf16[2,1024,3,128]{3,1,2,0:T(8,128)(2,1)S(1)}, bf16[2,1024,3,128]{3,1,2,0:T(8,128)(2,1)}, u32[]{:S(2)}) copy-start(bf16[2,1024,3,128]{3,1,2,0:T(8,128)(2,1)} %param.12) | copy-start | bytes 4718596
  37.9 2.0 %copy-start.2 = (f32[1024,1024]{1,0:T(8,128)}, f32[1024,1024]{1,0:T(8,128)S(1)}, u32[]{:S(2)}) copy-start(f32[1024,1024]{1,0:T(8,128)S(1)} %near.1.n_hbm) | copy-start | bytes 12582916
